TPU v7x, 32 devices: a whole 2x2x4 slice. The times are simulated.
32 devices in a mesh: by: 4 (over y, core), bz: 8 (over z, x).
Axes of the slice: x: 2, y: 2, z: 4, core: 2. Of those that a mesh axis runs over, the one named last changes fastest.
Arguments:
- fields: float32 [8, 64, 256, 512], P(None, 'by', 'bz'), may hold values from -400 to 400
- conductance: float32 [64, 256, 512], P('by', 'bz'), may hold values from 0.05 to 1
Outputs:
- basis: float32 [8, 64, 256, 512], P(None, 'by', 'bz')
- factor: float32 [512, 512], replicated
All inputs are finite; a program needn't handle non-finite values.
Results may differ from a plain program's by a relative error of at most 0.0003.
Values sent between devices are 32-bit elements; how exact they have to be, the bound alone decides.
A program may use at most 320 MiB of HBM per device.

v0:
```python
import jax
import jax.numpy as jnp
from jax import lax
from jax.sharding import PartitionSpec as P


def with_halo(cells, sides, width):
    for axis, dim in sides:
        count = lax.axis_size(axis)
        ends = count - 1
        head = lax.slice_in_dim(cells, 0, width, axis=dim)
        tail = lax.slice_in_dim(cells, cells.shape[dim] - width, cells.shape[dim], axis=dim)
        cells = jnp.concatenate(
            [
                lax.ppermute(tail, axis, [(i, (i + 1) % count) for i in range(ends)]),
                cells,
                lax.ppermute(head, axis, [((i + 1) % count, i) for i in range(ends)]),
            ],
            axis=dim,
        )
    return cells


def relax_inner(field_ext, cond_ext):
    centre = field_ext[:, 1:-1, 1:-1, :]
    kc = cond_ext[1:-1, 1:-1, :]
    total = jnp.zeros_like(centre)
    for nb, kn in (
        (field_ext[:, 2:, 1:-1, :], cond_ext[2:, 1:-1, :]),
        (field_ext[:, :-2, 1:-1, :], cond_ext[:-2, 1:-1, :]),
        (field_ext[:, 1:-1, 2:, :], cond_ext[1:-1, 2:, :]),
        (field_ext[:, 1:-1, :-2, :], cond_ext[1:-1, :-2, :]),
    ):
        total = total + jnp.sqrt(kc * kn)[None] * (nb - centre)
    padded = jnp.pad(centre, ((0, 0), (0, 0), (0, 0), (1, 1)))
    padk = jnp.pad(kc, ((0, 0), (0, 0), (1, 1)))
    total = total + jnp.sqrt(kc * padk[:, :, 2:])[None] * (padded[:, :, :, 2:] - centre)
    total = total + jnp.sqrt(kc * padk[:, :, :-2])[None] * (padded[:, :, :, :-2] - centre)
    return centre + 0.125 * total


def matmul_high(left, right):
    return jnp.dot(left, right, precision=lax.Precision.HIGHEST, preferred_element_type=jnp.float32)


def block_cholesky(block):
    size = block.shape[0]
    index = jnp.arange(size)

    def column_step(j, carry):
        work, lower = carry
        column = lax.dynamic_slice_in_dim(work, j, 1, 1)[:, 0]
        pivot = jnp.sqrt(lax.dynamic_slice_in_dim(column, j, 1, 0)[0])
        vector = jnp.where(index >= j, column / pivot, 0.0)
        lower = jnp.where(index[None, :] == j, vector[:, None], lower)
        work = work - vector[:, None] * vector[None, :]
        return (work, lower)

    start = (block, jnp.zeros_like(block))
    return lax.fori_loop(0, size, column_step, start)[1]


def block_lower_inverse(lower):
    size = lower.shape[0]
    index = jnp.arange(size)

    def row_step(i, inverse):
        row = lax.dynamic_slice_in_dim(lower, i, 1, 0)[0]
        pivot = lax.dynamic_slice_in_dim(row, i, 1, 0)[0]
        strict = jnp.where(index < i, row, 0.0)
        unit = jnp.where(index == i, 1.0, 0.0).astype(jnp.float32)
        value = (unit - matmul_high(strict[None, :], inverse)[0]) / pivot
        return jnp.where(index[:, None] == i, value[None, :], inverse)

    return lax.fori_loop(0, size, row_step, jnp.zeros_like(lower))


def factor_and_inverse(gram):
    width = gram.shape[0]
    step = min(width, 128)
    count = width // step
    work = gram
    lower = [[None] * count for _ in range(count)]
    diag_inv = []
    for k in range(count):
        lo = k * step
        lkk = block_cholesky(work[lo : lo + step, lo : lo + step])
        ikk = block_lower_inverse(lkk)
        lower[k][k] = lkk
        diag_inv.append(ikk)
        if k + 1 < count:
            panel = matmul_high(work[lo + step :, lo : lo + step], ikk.T)
            for i in range(k + 1, count):
                lower[i][k] = panel[(i - k - 1) * step : (i - k) * step]
            work = work.at[lo + step :, lo + step :].add(-matmul_high(panel, panel.T))
    zero = jnp.zeros((step, step), jnp.float32)
    full_lower = jnp.concatenate(
        [
            jnp.concatenate([lower[i][j] if j <= i else zero for j in range(count)], axis=1)
            for i in range(count)
        ],
        axis=0,
    )
    inv = [[None] * count for _ in range(count)]
    for k in range(count):
        inv[k][k] = diag_inv[k]
        for i in range(k + 1, count):
            acc = zero
            for j in range(k, i):
                acc = acc + matmul_high(lower[i][j], inv[j][k])
            inv[i][k] = -matmul_high(diag_inv[i], acc)
    lower_inverse = jnp.concatenate(
        [
            jnp.concatenate([inv[i][j] if j <= i else zero for j in range(count)], axis=1)
            for i in range(count)
        ],
        axis=0,
    )
    return (full_lower.T, lower_inverse.T)


def on_device(fields, conductance):
    nfield = fields.shape[0]
    width = fields.shape[3]
    stacked = jnp.concatenate([fields, conductance[None]], axis=0)
    extended = with_halo(stacked, (("by", 1), ("bz", 2)), 1)
    once = relax_inner(extended[:nfield], extended[nfield])
    again = with_halo(once, (("by", 1), ("bz", 2)), 1)
    relaxed = relax_inner(again, extended[nfield])
    total_rows = (
        nfield * fields.shape[1] * lax.axis_size("by") * fields.shape[2] * lax.axis_size("bz")
    )
    rows = relaxed.reshape(-1, width)
    local_gram = lax.dot_general(
        rows,
        rows,
        (((0,), (0,)), ((), ())),
        precision=lax.Precision.HIGHEST,
        preferred_element_type=jnp.float32,
    )
    local_gram = local_gram / jnp.float32(total_rows)
    gram = lax.psum(local_gram, ("by", "bz"))
    factor, inverse = factor_and_inverse(gram)
    basis = matmul_high(rows, inverse)
    return (basis.reshape(relaxed.shape), factor)


def solution(mesh):
    return jax.shard_map(
        on_device,
        mesh=mesh,
        in_specs=(P(None, "by", "bz", None), P("by", "bz", None)),
        out_specs=(P(None, "by", "bz", None), P()),
        check_vma=False,
    )
```

profile of v0, /device:TPU:0, one launch (start us, length us, event | category | flops | bytes accessed | tf_op | source)
XLA Modules:
  0.0 1861.1 jit_solution(13591025739690643991)
XLA Ops:
  7.2 1.5 pad_maximum_fusion.31
  8.8 2.7 collective-permute-start
  11.5 1.3 collective-permute-start.1
  13.0 4.4 collective-permute-done.1
  18.2 3.4 collective-permute-start.2
  21.6 1.3 collective-permute-start.3
  22.9 9.2 collective-permute-done.2
  34.2 2.4 fusion.129
  36.6 2.0 fusion.111
  38.6 35.8 %fusion.73 = f32[8,16,32,512]{3,2,1,0:T(8,128)} fusion(f32[8,16,32,512]{3,2,1,0:T(8,128)} %param.24, f32[9,18,1,512]{3,2,1,0:T(1,128)} %copy-done.5, f32[9,1,32,512]{3,2,1,0:T(8,128)} %copy-done.4, f32[9,1,32,512]{3,2,1,0:T(8,128)} %copy-done.3, f32[1,16,32,512]{3,2,1,0:T(8,128)S(1)} %bitcast.218, f32[9,18,1,512]{3,2,1,0:T(1,128)} %copy-done.6, ...), kind=kLoop, calls=%fused_computation.105 | loop fusion | flops 65011712 | bytes 25960448 | tf_op jit(solution)/shard_map/add | solution.py:39
  74.5 1.4 fusion.168
  75.9 1.3 collective-permute-start.4
  77.2 12.1 collective-permute-start.5
  89.3 1.5 collective-permute-done.5
  90.8 3.0 pad_maximum_fusion.38
  93.9 1.3 collective-permute-start.6
  95.3 4.7 collective-permute-start.7
  100.0 2.7 collective-permute-done.6
  102.7 1.0 copy.54
  103.7 6.5 collective-permute-done.7
  110.2 1.0 copy.56
  111.3 32.1 %fusion.81 = f32[8,16,32,512]{3,2,1,0:T(8,128)} fusion(f32[8,16,32,512]{3,2,1,0:T(8,128)} %fusion.73, f32[8,18,1,512]{3,2,1,0:T(1,128)} %copy.56, f32[8,1,32,512]{3,2,1,0:T(8,128)} %copy-done.7, f32[8,1,32,512]{3,2,1,0:T(8,128)} %copy-done.8, f32[8,18,1,512]{3,2,1,0:T(1,128)} %copy.54, f32[16,32,512]{2,1,0:T(8,128)} %get-tuple-element.1420, ...), kind=kLoop, calls=%fused_computation.113 | loop fusion | flops 56623104 | bytes 24707072 | tf_op jit(solution)/shard_map/add | solution.py:39
  143.4 17.3 fusion.107
  160.8 134.6 %all-reduce.7.cloned.1.call-done = f32[512,512]{1,0:T(8,128)} async-done(((f32[512,512]{1,0:T(8,128)}), f32[512,512]{1,0:T(8,128)}) %all-reduce.7.cloned.1.call-update) | async-done | bytes 1048592 | tf_op jit(solution)/shard_map/psum | solution.py:142
  295.4 0.8 slice.269
  296.4 187.0 %while.155 = (s32[]{:T(128)}, f32[128,128]{0,1:T(8,128)S(1)}, f32[128,128]{0,1:T(8,128)S(1)}, s32[]{:T(128)}, s32[]{:T(128)}, /*index=5*/s32[]{:T(128)}) while((s32[]{:T(128)}, f32[128,128]{0,1:T(8,128)S(1)}, f32[128,128]{0,1:T(8,128)S(1)}, s32[]{:T(128)}, s32[]{:T(128)}, /*index=5*/s32[]{:T(128)}) %tuple.411), condition=%wide.region_2.3_spmd.clone.clone, body=%wide.region_1.2_spmd.clone.clone.sunk | while | flops 66308 | bytes 267643 | solution.py:60
  483.5 195.4 %while.156 = (s32[]{:T(128)}, f32[128,128]{1,0:T(8,128)S(1)}, f32[128,128]{1,0:T(8,128)S(1)}, s32[]{:T(128)}, s32[]{:T(128)}, /*index=5*/s32[]{:T(128)}) while((s32[]{:T(128)}, f32[128,128]{1,0:T(8,128)S(1)}, f32[128,128]{1,0:T(8,128)S(1)}, s32[]{:T(128)}, s32[]{:T(128)}, /*index=5*/s32[]{:T(128)}) %tuple.414), condition=%wide.region_4.5_spmd.clone.clone, body=%wide.region_3.4_spmd.clone.clone.sunk | while | flops 246660 | bytes 200560 | solution.py:75
  485.6 0.8 fusion.228
  487.1 0.8 fusion.228
  488.7 0.8 fusion.228
  499.3 0.8 fusion.228
  500.9 0.8 fusion.228
  502.4 0.8 fusion.228
  503.9 0.8 fusion.228
  514.6 0.8 fusion.228
  516.1 0.8 fusion.228
  517.7 0.8 fusion.228
  528.4 0.8 fusion.228
  678.9 1.3 fusion.147
  680.2 1.7 slice_add_fusion
  682.1 186.9 %while.157 = (s32[]{:T(128)}, f32[128,128]{0,1:T(8,128)S(1)}, f32[128,128]{0,1:T(8,128)S(1)}, s32[]{:T(128)}, s32[]{:T(128)}, /*index=5*/s32[]{:T(128)}) while((s32[]{:T(128)}, f32[128,128]{0,1:T(8,128)S(1)}, f32[128,128]{0,1:T(8,128)S(1)}, s32[]{:T(128)}, s32[]{:T(128)}, /*index=5*/s32[]{:T(128)}) %tuple.417), condition=%wide.region_6.7_spmd.clone.clone, body=%wide.region_5.6_spmd.clone.clone.sunk | while | flops 66308 | bytes 267643 | solution.py:60
  869.1 195.4 %while.158 = (s32[]{:T(128)}, f32[128,128]{1,0:T(8,128)S(1)}, f32[128,128]{1,0:T(8,128)S(1)}, s32[]{:T(128)}, s32[]{:T(128)}, /*index=5*/s32[]{:T(128)}) while((s32[]{:T(128)}, f32[128,128]{1,0:T(8,128)S(1)}, f32[128,128]{1,0:T(8,128)S(1)}, s32[]{:T(128)}, s32[]{:T(128)}, /*index=5*/s32[]{:T(128)}) %tuple.420), condition=%wide.region_8.9_spmd.clone.clone, body=%wide.region_7.8_spmd.clone.clone.sunk | while | flops 246660 | bytes 200560 | solution.py:75
  1066.9 187.0 %while.159 = (s32[]{:T(128)}, f32[128,128]{0,1:T(8,128)S(1)}, f32[128,128]{0,1:T(8,128)S(1)}, s32[]{:T(128)}, s32[]{:T(128)}, /*index=5*/s32[]{:T(128)}) while((s32[]{:T(128)}, f32[128,128]{0,1:T(8,128)S(1)}, f32[128,128]{0,1:T(8,128)S(1)}, s32[]{:T(128)}, s32[]{:T(128)}, /*index=5*/s32[]{:T(128)}) %tuple.423), condition=%wide.region_10.11_spmd.clone.clone, body=%wide.region_9.10_spmd.clone.clone.sunk | while | flops 66308 | bytes 267643 | solution.py:60
  1254.0 195.4 %while.160 = (s32[]{:T(128)}, f32[128,128]{1,0:T(8,128)S(1)}, f32[128,128]{1,0:T(8,128)S(1)}, s32[]{:T(128)}, s32[]{:T(128)}, /*index=5*/s32[]{:T(128)}) while((s32[]{:T(128)}, f32[128,128]{1,0:T(8,128)S(1)}, f32[128,128]{1,0:T(8,128)S(1)}, s32[]{:T(128)}, s32[]{:T(128)}, /*index=5*/s32[]{:T(128)}) %tuple.426), condition=%wide.region_12.13_spmd.clone.clone, body=%wide.region_11.12_spmd.clone.clone.sunk | while | flops 246660 | bytes 200560 | solution.py:75
  1450.7 187.0 %while.161 = (s32[]{:T(128)}, f32[128,128]{0,1:T(8,128)S(1)}, f32[128,128]{0,1:T(8,128)S(1)}, s32[]{:T(128)}, s32[]{:T(128)}, /*index=5*/s32[]{:T(128)}) while((s32[]{:T(128)}, f32[128,128]{0,1:T(8,128)S(1)}, f32[128,128]{0,1:T(8,128)S(1)}, s32[]{:T(128)}, s32[]{:T(128)}, /*index=5*/s32[]{:T(128)}) %tuple.429), condition=%wide.region_14.15_spmd.clone.clone, body=%wide.region_13.14_spmd.clone.clone.sunk | while | flops 66308 | bytes 267643 | solution.py:60
  1639.0 195.7 %while.162 = (s32[]{:T(128)}, f32[128,128]{1,0:T(8,128)S(1)}, f32[128,128]{1,0:T(8,128)S(1)}, s32[]{:T(128)}, s32[]{:T(128)}, /*index=5*/s32[]{:T(128)}) while((s32[]{:T(128)}, f32[128,128]{1,0:T(8,128)S(1)}, f32[128,128]{1,0:T(8,128)S(1)}, s32[]{:T(128)}, s32[]{:T(128)}, /*index=5*/s32[]{:T(128)}) %tuple.432), condition=%wide.region_16.17_spmd.clone.clone, body=%wide.region_15.16_spmd.clone.clone.sunk | while | flops 246660 | bytes 200560 | solution.py:75
  1836.6 1.1 fusion.123
  1837.6 16.7 fusion.118
  (4673 shorter events, 1132.3 us)
Async XLA Ops:
  7.2 10.3 copy-start.1
  7.2 288.2 %all-reduce.7.cloned.1.call-start = ((), (), s32[]{:S(2)}) async-start(), calls=%async_computation | async-start | bytes 2097152 | tf_op jit(solution)/shard_map/psum | solution.py:142
  7.2 10.2 copy-start
  8.8 4.2 collective-permute-start
  11.5 6.0 collective-permute-start.1
  13.0 21.1 %copy-start.3 = (f32[9,1,32,512]{3,2,1,0:T(8,128)}, f32[9,1,32,512]{3,2,1,0:T(8,128)S(1)}, u32[]{:S(2)}) copy-start(f32[9,1,32,512]{3,2,1,0:T(8,128)S(1)} %collective-permute-done) | copy-start | bytes 1769476
  17.5 16.7 copy-start.4
  18.2 14.0 collective-permute-start.2
  21.6 10.9 collective-permute-start.3
  32.5 0.7 copy-start.5
  33.2 0.7 copy-start.6
  74.5 36.8 %copy-start.2 = (f32[16,32,512]{2,1,0:T(8,128)S(1)}, f32[16,32,512]{2,1,0:T(8,128)}, u32[]{:S(2)}) copy-start(f32[16,32,512]{2,1,0:T(8,128)} %get-tuple-element.1416) | copy-start | bytes 3145732
  75.9 13.4 collective-permute-start.4
  77.2 13.6 collective-permute-start.5
  89.3 1.5 copy-start.7
  90.8 3.0 copy-start.8
  93.9 8.8 collective-permute-start.6
  95.3 15.0 collective-permute-start.7
Sparse Core Ops, SparseCore 0:
  160.8 134.5 all-reduce.6
where the time goes:
time: 1880 us; the launch traced here: 1860 us
  local copies, waits for them, and re-layouts  610 us (32%)
  matrix products  452 us (24%)
  loops' own time  399 us (21%)
  other arithmetic  198 us (11%)
  waiting for transfers between devices  159 us (8%)
  starting transfers between devices  28.1 us (1%)
    dot_general x535, matrix products, matmul_high(): jnp.dot(left, right, precision=lax.Precision.HIGHEST, preferred_element_t...  435 us
    another operation x4, loops' own time, block_cholesky(): return lax.fori_loop(0, size, column_step, start)[1]  382 us
    dynamic_slice x512, local copies, waits for them, and re-layouts, row_step(): pivot = lax.dynamic_slice_in_dim(row, i, 1, 0)[0]  301 us
    dynamic_slice x512, local copies, waits for them, and re-layouts, column_step(): pivot = jnp.sqrt(lax.dynamic_slice_in_dim(column, j, 1, 0)[0])  301 us
    psum x1, waiting for transfers between devices, on_device(): gram = lax.psum(local_gram, ('by', 'bz'))  135 us
    add x2, other arithmetic, relax_inner(): return centre + 0.125 * total  67.9 us
    select_n x512, other arithmetic, column_step(): lower = jnp.where(index[None, :] == j, vector[:, None], lower)  53.1 us
    select_n x512, other arithmetic, row_step(): return jnp.where(index[:, None] == i, value[None, :], inverse)  45.5 us

commit v1 on v0

v1 whole, which is shorter than its diff:
```python
import functools

import jax
import jax.numpy as jnp
from jax import lax
from jax.experimental import pallas as pl
from jax.experimental.pallas import tpu as pltpu
from jax.sharding import PartitionSpec as P

VMEM_LIMIT = 58 * 1024 * 1024
HIGHEST = lax.Precision.HIGHEST
HIGH = lax.Precision.HIGH
STEP = 128


def shift_faces(cells, axis):
    count = lax.axis_size(axis)
    head, tail = cells
    below = lax.ppermute(tail, axis, [(i, i + 1) for i in range(count - 1)])
    above = lax.ppermute(head, axis, [(i + 1, i) for i in range(count - 1)])
    return below, above


def relax_kernel(with_faces, u_ref, k_ref, yb_ref, ya_ref, zb_ref, za_ref, kyb_ref, kya_ref, kzb_ref, kza_ref, *rest):
    if with_faces:
        out_ref, ylo_ref, yhi_ref, zlo_ref, zhi_ref, ext, root = rest
    else:
        out_ref, ext, root = rest
    nf, ny, nz, nx = u_ref.shape
    top = 8 + nz

    def fill_root(y, carry):
        root[y + 1, pl.ds(8, nz), :] = jnp.sqrt(k_ref[y])
        return carry

    lax.fori_loop(0, ny, fill_root, 0)
    root[0, pl.ds(8, nz), :] = jnp.sqrt(kyb_ref[...])
    root[ny + 1, pl.ds(8, nz), :] = jnp.sqrt(kya_ref[...])
    root[pl.ds(1, ny), 7:8, :] = jnp.sqrt(kzb_ref[...])[:, None, :]
    root[pl.ds(1, ny), top : top + 1, :] = jnp.sqrt(kza_ref[...])[:, None, :]

    def fill(f, carry):
        def fill_y(y, c):
            ext[f, y + 1, pl.ds(8, nz), :] = u_ref[f, y]
            return c

        lax.fori_loop(0, ny, fill_y, 0)
        ext[f, 0, pl.ds(8, nz), :] = yb_ref[f]
        ext[f, ny + 1, pl.ds(8, nz), :] = ya_ref[f]
        ext[f, pl.ds(1, ny), 7:8, :] = zb_ref[f][:, None, :]
        ext[f, pl.ds(1, ny), top : top + 1, :] = za_ref[f][:, None, :]
        return carry

    lax.fori_loop(0, nf, fill, 0)

    lane = lax.broadcasted_iota(jnp.int32, (8, nx), 1)

    def plane(y, carry):
        for z in range(0, nz, 8):
            centre = 0.125 * root[y + 1, pl.ds(8 + z, 8), :]
            plain = root[y + 1, pl.ds(8 + z, 8), :]
            wyp = centre * root[y + 2, pl.ds(8 + z, 8), :]
            wym = centre * root[y, pl.ds(8 + z, 8), :]
            wzp = centre * root[y + 1, pl.ds(9 + z, 8), :]
            wzm = centre * root[y + 1, pl.ds(7 + z, 8), :]
            wxp = jnp.where(lane == nx - 1, 0.0, centre * pltpu.roll(plain, nx - 1, 1))
            wxm = jnp.where(lane == 0, 0.0, centre * pltpu.roll(plain, 1, 1))
            keep = 1.0 - (((wyp + wym) + (wzp + wzm)) + (wxp + wxm))
            for f in range(nf):
                mid = ext[f, y + 1, pl.ds(8 + z, 8), :]
                near = wyp * ext[f, y + 2, pl.ds(8 + z, 8), :] + wym * ext[f, y, pl.ds(8 + z, 8), :]
                side = wzp * ext[f, y + 1, pl.ds(9 + z, 8), :] + wzm * ext[f, y + 1, pl.ds(7 + z, 8), :]
                along = wxp * pltpu.roll(mid, nx - 1, 1) + wxm * pltpu.roll(mid, 1, 1)
                out_ref[f, y, pl.ds(z, 8), :] = (keep * mid + near) + (side + along)
        return carry

    lax.fori_loop(0, ny, plane, 0)
    if with_faces:
        for f in range(nf):
            ylo_ref[f] = out_ref[f, 0]
            yhi_ref[f] = out_ref[f, ny - 1]
            zlo_ref[f] = out_ref[f, :, 0, :]
            zhi_ref[f] = out_ref[f, :, nz - 1, :]


def relax_call(u, k, faces, kfaces, with_faces):
    nf, ny, nz, nx = u.shape
    full = jax.ShapeDtypeStruct(u.shape, jnp.float32)
    yface = jax.ShapeDtypeStruct((nf, nz, nx), jnp.float32)
    zface = jax.ShapeDtypeStruct((nf, ny, nx), jnp.float32)
    outs = [full] + ([yface, yface, zface, zface] if with_faces else [])
    return pl.pallas_call(
        functools.partial(relax_kernel, with_faces),
        out_shape=outs,
        in_specs=[pl.BlockSpec(memory_space=pltpu.VMEM)] * 10,
        out_specs=[pl.BlockSpec(memory_space=pltpu.VMEM)] * len(outs),
        scratch_shapes=[
            pltpu.VMEM((nf, ny + 2, nz + 16, nx), jnp.float32),
            pltpu.VMEM((ny + 2, nz + 16, nx), jnp.float32),
        ],
        compiler_params=pltpu.CompilerParams(vmem_limit_bytes=VMEM_LIMIT),
        name="relax",
    )(u, k, *faces, *kfaces)


def eliminate(block):
    size = block.shape[0]
    groups = size // 8
    row8 = lax.broadcasted_iota(jnp.int32, (8, size), 0)
    lane8 = lax.broadcasted_iota(jnp.int32, (8, size), 1)
    work = [block[8 * g : 8 * g + 8] for g in range(groups)]
    side = [jnp.where(row8 + 8 * g == lane8, 1.0, 0.0) for g in range(groups)]
    for j in range(size):
        g, r = divmod(j, 8)
        spread = jnp.broadcast_to(work[g][:, j : j + 1], (8, size))
        inv = 1.0 / jnp.broadcast_to(spread[r : r + 1], (8, size))
        row = jnp.broadcast_to(work[g][r : r + 1], (8, size)) * inv
        arow = jnp.broadcast_to(side[g][r : r + 1], (8, size)) * inv
        for q in range(g, groups):
            if q == g:
                if r == 7:
                    continue
                mult = jnp.where(row8 > r, spread, 0.0)
            else:
                mult = jnp.broadcast_to(work[q][:, j : j + 1], (8, size))
            work[q] = work[q] - mult * row
            side[q] = side[q] - mult * arow
    return jnp.concatenate(work, axis=0), jnp.concatenate(side, axis=0)


def factor_kernel(gram_ref, factor_ref, inv_ref, work, side):
    n = gram_ref.shape[0]
    step = min(n, STEP)
    count = n // step
    big = (((1,), (0,)), ((), ()))
    tall = (((0,), (0,)), ((), ()))
    rows = lax.broadcasted_iota(jnp.int32, (step, step), 0)
    cols = lax.broadcasted_iota(jnp.int32, (step, step), 1)
    col_n = lax.broadcasted_iota(jnp.int32, (step, n), 1)
    row_n = lax.broadcasted_iota(jnp.int32, (step, n), 0)
    work[...] = gram_ref[...]
    side[...] = jnp.zeros_like(side)

    def block_step(k, carry):
        lo = pl.multiple_of(k * step, step)
        here = pl.ds(lo, step)
        upper, lower = eliminate(work[here, here])
        pivot = jnp.sum(jnp.where(rows == cols, upper, 0.0), axis=1, keepdims=True)
        scale = 1.0 / jnp.sqrt(pivot)
        linv = lower * scale
        solved = lax.dot_general(linv, work[here, :], big, precision=HIGHEST, preferred_element_type=jnp.float32)
        factor_ref[here, :] = jnp.where(col_n >= row_n + lo, solved, 0.0)
        factor_ref[here, here] = jnp.where(cols >= rows, upper * scale, 0.0)
        left = side[here, :]
        left = lax.dot_general(linv, left, big, precision=HIGHEST, preferred_element_type=jnp.float32)
        inv_ref[here, :] = left
        inv_ref[here, here] = linv

        def trail(i, c):
            there = pl.ds(pl.multiple_of(i * step, step), step)
            mult = factor_ref[here, there]
            work[there, :] -= lax.dot_general(mult, factor_ref[here, :], tall, precision=HIGHEST, preferred_element_type=jnp.float32)
            side[there, :] -= lax.dot_general(mult, inv_ref[here, :], tall, precision=HIGHEST, preferred_element_type=jnp.float32)
            return c

        lax.fori_loop(k + 1, count, trail, 0)
        return carry

    lax.fori_loop(0, count, block_step, 0)


def factor_call(gram):
    shape = jax.ShapeDtypeStruct(gram.shape, jnp.float32)
    return pl.pallas_call(
        factor_kernel,
        out_shape=[shape, shape],
        in_specs=[pl.BlockSpec(memory_space=pltpu.VMEM)],
        out_specs=[pl.BlockSpec(memory_space=pltpu.VMEM)] * 2,
        scratch_shapes=[pltpu.VMEM(gram.shape, jnp.float32)] * 2,
        compiler_params=pltpu.CompilerParams(vmem_limit_bytes=VMEM_LIMIT),
        name="factor",
    )(gram)


def on_device(fields, conductance):
    nf, ny, nz, nx = fields.shape
    total_rows = nf * ny * lax.axis_size("by") * nz * lax.axis_size("bz")
    stacked = lambda f, k: jnp.concatenate([f, k[None]], axis=0)
    yfaces = shift_faces(
        (stacked(fields[:, 0], conductance[0]), stacked(fields[:, ny - 1], conductance[ny - 1])), "by"
    )
    zfaces = shift_faces(
        (stacked(fields[:, :, 0], conductance[:, 0]), stacked(fields[:, :, nz - 1], conductance[:, nz - 1])), "bz"
    )
    faces = [a[:nf] for a in (*yfaces, *zfaces)]
    kfaces = [a[nf] for a in (*yfaces, *zfaces)]
    once, ylo, yhi, zlo, zhi = relax_call(fields, conductance, faces, kfaces, True)
    again = (*shift_faces((ylo, yhi), "by"), *shift_faces((zlo, zhi), "bz"))
    relaxed = relax_call(once, conductance, again, kfaces, False)[0]
    rows = relaxed.reshape(-1, nx)
    gram = lax.dot_general(
        rows, rows, (((0,), (0,)), ((), ())), precision=HIGH, preferred_element_type=jnp.float32
    )
    gram = lax.psum(gram / jnp.float32(total_rows), ("by", "bz"))
    factor, linv = factor_call(gram)
    basis = lax.dot_general(
        rows, linv, (((1,), (1,)), ((), ())), precision=HIGH, preferred_element_type=jnp.float32
    )
    return (basis.reshape(relaxed.shape), factor)


def solution(mesh):
    return jax.shard_map(
        on_device,
        mesh=mesh,
        in_specs=(P(None, "by", "bz", None), P("by", "bz", None)),
        out_specs=(P(None, "by", "bz", None), P()),
        check_vma=False,
    )
```

time: 1880 us -> 337 us (0.18)
  local copies, waits for them, and re-layouts: 610 us -> 12.8 us
  matrix products: 452 us -> 30.4 us
  loops' own time: 399 us -> 0 us
  other arithmetic: 198 us -> 0.13 us
  Pallas kernels: 0 us -> 109 us
    dynamic_slice x1024 -> x0, local copies, waits for them, and re-layouts: 602 us -> none  [the longest x512 301 us: row_step(): pivot = lax.dynamic_slice_in_dim(row, i, 1, 0)[0]]
    dot_general x536 -> x2, matrix products: 452 us -> 30.4 us  [the longest x1 19 us: on_device(): lax.dot_general(rows, rows, (((0,), (0,)), ((), ())), precision=HIGH, pre...]
    another operation x8 -> x0, loops' own time: 399 us -> none  [the longest x4 382 us: block_cholesky(): return lax.fori_loop(0, size, column_step, start)[1]]
    pallas_call x0 -> x3, Pallas kernels: none -> 109 us  [the longest x1 77.3 us: factor_call(): pl.pallas_call(factor_kernel, out_shape=[shape, shape], in_specs=[pl.Bloc...]
    select_n x1536 -> x0, other arithmetic: 101 us -> none  [the longest x512 53.1 us: column_step(): lower = jnp.where(index[None, :] == j, vector[:, None], lower)]
    add x2 -> x0, other arithmetic: 67.9 us -> none  [relax_inner(): return centre + 0.125 * total]
where the time goes in v1:
time: 337 us; the launch traced here: 336 us
  waiting for transfers between devices  149 us (44%)
  Pallas kernels  109 us (32%)
  matrix products  30.4 us (9%)
  starting transfers between devices  19.8 us (6%)
  between operations  14.2 us (4%)
  local copies, waits for them, and re-layouts  12.8 us (4%)
    psum x1, waiting for transfers between devices, on_device(): gram = lax.psum(gram / jnp.float32(total_rows), ('by', 'bz'))  133 us
    pallas_call x1, Pallas kernels, factor_call(): pl.pallas_call(factor_kernel, out_shape=[shape, shape], in_specs=[pl.Bloc...  77.3 us
    pallas_call x2, Pallas kernels, relax_call(): pl.pallas_call(functools.partial(relax_kernel, with_faces), out_shape=out...  32.1 us
    dot_general x1, matrix products, on_device(): lax.dot_general(rows, rows, (((0,), (0,)), ((), ())), precision=HIGH, pre...  19 us
    ppermute x4, starting transfers between devices, shift_faces(): below = lax.ppermute(tail, axis, [(i, i + 1) for i in range(count - 1)])  14.5 us
    ppermute x4, waiting for transfers between devices, shift_faces(): below = lax.ppermute(tail, axis, [(i, i + 1) for i in range(count - 1)])  11.5 us
    dot_general x1, matrix products, on_device(): lax.dot_general(rows, linv, (((1,), (1,)), ((), ())), precision=HIGH, pre...  11.4 us
  transfers between devices with their start and end apart: 9, of which 4 were waited for; matrix products, arithmetic and copies ran while one was open for 2% of the time, Pallas kernels for 0%

profile of v1, /device:TPU:0, one launch (start us, length us, event | category | flops | bytes accessed | tf_op | source)
XLA Modules:
  0.0 336.3 jit_solution(2450131140351423414)
XLA Ops:
  7.2 0.0 all-reduce.2.cloned.1.call-start
  7.2 1.1 fusion.4
  8.3 2.8 fusion.3
  11.1 4.9 %collective-permute-start.2 = (f32[9,16,512]{2,1,0:T(8,128)S(1)}, f32[9,16,512]{2,1,0:T(8,128)S(1)}, u32[]{:S(2)}, u32[]{:S(2)}) collective-permute-start(f32[9,16,512]{2,1,0:T(8,128)S(1)} %pad_maximum_fusion.2), channel_id=1, source_target_pairs={{0,1},{1,2},{2,3},{3,4},{4,5},{5,6},{6,7},{8,9},{9,10},{10,11},{11... | collective-permute-start | bytes 884744 | tf_op jit(solution)/shard_map/ppermute | solution.py:19
  16.1 1.3 collective-permute-start.3
  17.4 1.3 slice_bitcast_fusion
  18.7 0.9 fusion.5
  19.6 1.5 collective-permute-start
  21.2 1.3 collective-permute-start.1
  22.5 6.1 %collective-permute-done.2 = f32[9,16,512]{2,1,0:T(8,128)S(1)} collective-permute-done((f32[9,16,512]{2,1,0:T(8,128)S(1)}, f32[9,16,512]{2,1,0:T(8,128)S(1)}, u32[]{:S(2)}, u32[]{:S(2)}) %collective-permute-start.2) | collective-permute-done | bytes 294944 | tf_op jit(solution)/shard_map/ppermute | solution.py:19
  28.6 0.7 slice.66.zb_ref
  29.3 0.0 collective-permute-done.3
  29.3 0.7 slice.67.za_ref
  30.0 0.6 slice_bitcast_fusion.5.kzb_ref
  30.6 0.6 slice_bitcast_fusion.4.kza_ref
  31.2 0.0 collective-permute-done
  31.2 0.8 slice.64.yb_ref
  32.1 0.6 slice_bitcast_fusion.3.kyb_ref
  32.7 0.0 collective-permute-done.1
  32.7 0.6 slice_bitcast_fusion.2.kya_ref
  33.3 0.9 slice.65.ya_ref
  34.2 16.4 %relax.2 = (f32[8,16,32,512]{3,2,1,0:T(8,128)}, f32[8,32,512]{2,1,0:T(8,128)}, f32[8,32,512]{2,1,0:T(8,128)}, f32[8,16,512]{2,1,0:T(8,128)}, f32[8,16,512]{2,1,0:T(8,128)}) custom-call(f32[8,16,32,512]{3,2,1,0:T(8,128)} %u_ref.1, f32[16,32,512]{2,1,0:T(8,128)} %k_ref.3, f32[8,32,512]{2,1,0:T(8,128)} %slice.64.yb_ref, f32[8,32,512]{2,1,0:T(8,128)} %slice.65.ya_ref, ...), custom_call_target="tpu_custom_call" | custom-call | tf_op jit(solution)/shard_map/relax/pallas_call | solution.py:92
  50.6 3.6 %collective-permute-start.4 = (f32[8,32,512]{2,1,0:T(8,128)}, f32[8,32,512]{2,1,0:T(8,128)S(1)}, u32[]{:S(2)}, u32[]{:S(2)}) collective-permute-start(f32[8,32,512]{2,1,0:T(8,128)} %get-tuple-element.10), channel_id=1, source_target_pairs={{0,8},{8,16},{16,24},{1,9},{9,17},{17,25},{2,10},{10,18},{18,26},{... | collective-permute-start | bytes 1572872 | tf_op jit(solution)/shard_map/ppermute | solution.py:19
  54.2 1.3 collective-permute-start.5
  55.5 4.6 %collective-permute-start.6 = (f32[8,16,512]{2,1,0:T(8,128)}, f32[8,16,512]{2,1,0:T(8,128)S(1)}, u32[]{:S(2)}, u32[]{:S(2)}) collective-permute-start(f32[8,16,512]{2,1,0:T(8,128)} %get-tuple-element.12), channel_id=1, source_target_pairs={{0,1},{1,2},{2,3},{3,4},{4,5},{5,6},{6,7},{8,9},{9,10},{10,11},{11... | collective-permute-start | bytes 786440 | tf_op jit(solution)/shard_map/ppermute | solution.py:19
  60.1 1.3 collective-permute-start.7
  61.4 5.4 %collective-permute-done.6.zb_ref = f32[8,16,512]{2,1,0:T(8,128)S(1)} collective-permute-done((f32[8,16,512]{2,1,0:T(8,128)}, f32[8,16,512]{2,1,0:T(8,128)S(1)}, u32[]{:S(2)}, u32[]{:S(2)}) %collective-permute-start.6) | collective-permute-done | bytes 262176 | tf_op jit(solution)/shard_map/ppermute | solution.py:19
  66.8 0.0 copy-start.2
  66.8 4.8 %collective-permute-done.7.za_ref = f32[8,16,512]{2,1,0:T(8,128)S(1)} collective-permute-done((f32[8,16,512]{2,1,0:T(8,128)}, f32[8,16,512]{2,1,0:T(8,128)S(1)}, u32[]{:S(2)}, u32[]{:S(2)}) %collective-permute-start.7) | collective-permute-done | bytes 262176 | tf_op jit(solution)/shard_map/ppermute | solution.py:20
  71.6 0.0 copy-start.3
  71.7 0.0 collective-permute-done.4.yb_ref
  71.7 0.0 copy-start
  71.7 0.0 collective-permute-done.5.ya_ref
  71.7 0.0 copy-start.1
  71.7 0.0 copy-done.2
  71.7 0.7 copy-done.3
  72.3 0.2 copy-done
  72.5 0.2 copy-done.1
  72.7 15.7 %relax.3 = f32[8,16,32,512]{3,2,1,0:T(8,128)} custom-call(f32[8,16,32,512]{3,2,1,0:T(8,128)} %get-tuple-element.9.u_ref, f32[16,32,512]{2,1,0:T(8,128)} %k_ref.3, f32[8,32,512]{2,1,0:T(8,128)} %copy-done, f32[8,32,512]{2,1,0:T(8,128)} %copy-done.1, f32[8,16,512]{2,1,0:T(8,128)} %copy-done.2, f32[8,16,512]{2,1,0:T(8,128)} %copy-done.3, ...), custom_call_target="tpu_custom_call" | custom-call | tf_op jit(solution)/shard_map/relax/pallas_call | solution.py:92
  88.5 19.0 %fusion = f32[512,512]{1,0:T(8,128)} fusion(f32[8,16,32,512]{3,2,1,0:T(8,128)} %relax.3), kind=kOutput, calls=%fused_computation.1 | convolution fusion | flops 6442713088 | bytes 9437184 | tf_op jit(solution)/shard_map/dot_general | solution.py:201
  107.5 0.0 all-reduce.2.cloned.1.call-update
  107.5 133.1 %all-reduce.2.cloned.1.call-done.gram_ref = f32[512,512]{1,0:T(8,128)} async-done(((f32[512,512]{1,0:T(8,128)}), f32[512,512]{1,0:T(8,128)}) %all-reduce.2.cloned.1.call-update) | async-done | bytes 1048592 | tf_op jit(solution)/shard_map/psum | solution.py:204
  240.6 77.3 %factor.1 = (f32[512,512]{1,0:T(8,128)}, f32[512,512]{1,0:T(8,128)}) custom-call(f32[512,512]{1,0:T(8,128)} %all-reduce.2.cloned.1.call-done.gram_ref), custom_call_target="tpu_custom_call" | custom-call | tf_op jit(solution)/shard_map/factor/pallas_call | solution.py:174
  318.0 11.4 %fusion.1 = f32[8,16,32,512]{3,2,1,0:T(8,128)} fusion(f32[8,16,32,512]{3,2,1,0:T(8,128)} %relax.3, f32[512,512]{1,0:T(8,128)} %get-tuple-element.14), kind=kOutput, calls=%fused_computation.2 | convolution fusion | flops 6442450944 | bytes 17825792 | tf_op jit(solution)/shard_map/dot_general | solution.py:206
  (8 shorter events, 0.2 us)
Async XLA Ops:
  7.2 233.4 %all-reduce.2.cloned.1.call-start = ((), (), s32[]{:S(2)}) async-start(), calls=%async_computation | async-start | bytes 2097152 | tf_op jit(solution)/shard_map/psum | solution.py:204
  11.1 17.4 %collective-permute-start.2 = (f32[9,16,512]{2,1,0:T(8,128)S(1)}, f32[9,16,512]{2,1,0:T(8,128)S(1)}, u32[]{:S(2)}, u32[]{:S(2)}) collective-permute-start(f32[9,16,512]{2,1,0:T(8,128)S(1)} %pad_maximum_fusion.2), channel_id=1, source_target_pairs={{0,1},{1,2},{2,3},{3,4},{4,5},{5,6},{6,7},{8,9},{9,10},{10,11},{11... | collective-permute-start | bytes 884744 | tf_op jit(solution)/shard_map/ppermute | solution.py:19
  16.1 13.2 %collective-permute-start.3 = (f32[9,16,512]{2,1,0:T(8,128)S(1)}, f32[9,16,512]{2,1,0:T(8,128)S(1)}, u32[]{:S(2)}, u32[]{:S(2)}) collective-permute-start(f32[9,16,512]{2,1,0:T(8,128)S(1)} %pad_maximum_fusion.3), channel_id=1, source_target_pairs={{1,0},{2,1},{3,2},{4,3},{5,4},{6,5},{7,6},{9,8},{10,9},{11,10},{12... | collective-permute-start | bytes 884744 | tf_op jit(solution)/shard_map/ppermute | solution.py:20
  19.6 11.6 %collective-permute-start = (f32[9,32,512]{2,1,0:T(8,128)S(1)}, f32[9,32,512]{2,1,0:T(8,128)S(1)}, u32[]{:S(2)}, u32[]{:S(2)}) collective-permute-start(f32[9,32,512]{2,1,0:T(8,128)S(1)} %pad_maximum_fusion), channel_id=1, source_target_pairs={{0,8},{8,16},{16,24},{1,9},{9,17},{17,25},{2,10},{10,18},{18,26},{... | collective-permute-start | bytes 1769480 | tf_op jit(solution)/shard_map/ppermute | solution.py:19
  21.2 11.5 %collective-permute-start.1 = (f32[9,32,512]{2,1,0:T(8,128)S(1)}, f32[9,32,512]{2,1,0:T(8,128)S(1)}, u32[]{:S(2)}, u32[]{:S(2)}) collective-permute-start(f32[9,32,512]{2,1,0:T(8,128)S(1)} %pad_maximum_fusion.1), channel_id=1, source_target_pairs={{8,0},{16,8},{24,16},{9,1},{17,9},{25,17},{10,2},{18,10},{26,18},{... | collective-permute-start | bytes 1769480 | tf_op jit(solution)/shard_map/ppermute | solution.py:20
  50.6 21.0 %collective-permute-start.4 = (f32[8,32,512]{2,1,0:T(8,128)}, f32[8,32,512]{2,1,0:T(8,128)S(1)}, u32[]{:S(2)}, u32[]{:S(2)}) collective-permute-start(f32[8,32,512]{2,1,0:T(8,128)} %get-tuple-element.10), channel_id=1, source_target_pairs={{0,8},{8,16},{16,24},{1,9},{9,17},{17,25},{2,10},{10,18},{18,26},{... | collective-permute-start | bytes 1572872 | tf_op jit(solution)/shard_map/ppermute | solution.py:19
  54.2 17.4 %collective-permute-start.5 = (f32[8,32,512]{2,1,0:T(8,128)}, f32[8,32,512]{2,1,0:T(8,128)S(1)}, u32[]{:S(2)}, u32[]{:S(2)}) collective-permute-start(f32[8,32,512]{2,1,0:T(8,128)} %get-tuple-element.11), channel_id=1, source_target_pairs={{8,0},{16,8},{24,16},{9,1},{17,9},{25,17},{10,2},{18,10},{26,18},{... | collective-permute-start | bytes 1572872 | tf_op jit(solution)/shard_map/ppermute | solution.py:20
  55.5 11.3 %collective-permute-start.6 = (f32[8,16,512]{2,1,0:T(8,128)}, f32[8,16,512]{2,1,0:T(8,128)S(1)}, u32[]{:S(2)}, u32[]{:S(2)}) collective-permute-start(f32[8,16,512]{2,1,0:T(8,128)} %get-tuple-element.12), channel_id=1, source_target_pairs={{0,1},{1,2},{2,3},{3,4},{4,5},{5,6},{6,7},{8,9},{9,10},{10,11},{11... | collective-permute-start | bytes 786440 | tf_op jit(solution)/shard_map/ppermute | solution.py:19
  60.1 11.5 %collective-permute-start.7 = (f32[8,16,512]{2,1,0:T(8,128)}, f32[8,16,512]{2,1,0:T(8,128)S(1)}, u32[]{:S(2)}, u32[]{:S(2)}) collective-permute-start(f32[8,16,512]{2,1,0:T(8,128)} %get-tuple-element.13), channel_id=1, source_target_pairs={{1,0},{2,1},{3,2},{4,3},{5,4},{6,5},{7,6},{9,8},{10,9},{11,10},{12... | collective-permute-start | bytes 786440 | tf_op jit(solution)/shard_map/ppermute | solution.py:20
  66.8 4.9 %copy-start.2 = (f32[8,16,512]{2,1,0:T(8,128)}, f32[8,16,512]{2,1,0:T(8,128)S(1)}, u32[]{:S(2)}) copy-start(f32[8,16,512]{2,1,0:T(8,128)S(1)} %collective-permute-done.6.zb_ref) | copy-start | bytes 786436
  71.6 0.7 copy-start.3
  71.7 0.9 copy-start
  71.7 1.1 copy-start.1
Sparse Core Ops, SparseCore 0:
  107.6 132.9 all-reduce.1

commit v2 on v1

--- a/solution.py
+++ b/solution.py
@@ -21,11 +21,16 @@
     return below, above
 
 
-def relax_kernel(with_faces, u_ref, k_ref, yb_ref, ya_ref, zb_ref, za_ref, kyb_ref, kya_ref, kzb_ref, kza_ref, *rest):
+def upper_blocks(n):
+    count = n // STEP
+    return [(i, j) for i in range(count) for j in range(i, count)]
+
+
+def relax_kernel(with_faces, total_rows, u_ref, k_ref, yb_ref, ya_ref, zb_ref, za_ref, kyb_ref, kya_ref, kzb_ref, kza_ref, *rest):
     if with_faces:
         out_ref, ylo_ref, yhi_ref, zlo_ref, zhi_ref, ext, root = rest
     else:
-        out_ref, ext, root = rest
+        out_ref, gram_ref, ext, root, head, cross = rest
     nf, ny, nz, nx = u_ref.shape
     top = 8 + nz
 
@@ -81,26 +86,61 @@
             yhi_ref[f] = out_ref[f, ny - 1]
             zlo_ref[f] = out_ref[f, :, 0, :]
             zhi_ref[f] = out_ref[f, :, nz - 1, :]
-
-
-def relax_call(u, k, faces, kfaces, with_faces):
+    else:
+        pack_gram(total_rows, out_ref, gram_ref, head, cross)
+
+
+def pack_gram(total_rows, rows_ref, gram_ref, head, cross):
+    nf, ny, nz, nx = rows_ref.shape
+    half = nx // 2
+    tall = (((0,), (0,)), ((), ()))
+    head[...] = jnp.zeros_like(head)
+    cross[...] = jnp.zeros_like(cross)
+
+    def add(f, carry):
+        x = rows_ref[f].reshape(ny * nz, nx)
+        hi = x.astype(jnp.bfloat16)
+        lo = (x - hi.astype(jnp.float32)).astype(jnp.bfloat16)
+        for c in range(2):
+            cols = slice(c * half, (c + 1) * half)
+            left = hi[:, cols]
+            cross[cols, :] += lax.dot_general(left, lo, tall, preferred_element_type=jnp.float32)
+            head[cols, c * half :] += lax.dot_general(left, hi[:, c * half :], tall, preferred_element_type=jnp.float32)
+        return carry
+
+    lax.fori_loop(0, nf, add, 0)
+    for b, (i, j) in enumerate(upper_blocks(nx)):
+        ri, rj = slice(i * STEP, (i + 1) * STEP), slice(j * STEP, (j + 1) * STEP)
+        total = head[ri, rj] + (cross[ri, rj] + cross[rj, ri].T)
+        gram_ref[b * STEP : (b + 1) * STEP, :] = total / jnp.float32(total_rows)
+
+
+def relax_call(u, k, faces, kfaces, with_faces, total_rows=1):
     nf, ny, nz, nx = u.shape
     full = jax.ShapeDtypeStruct(u.shape, jnp.float32)
     yface = jax.ShapeDtypeStruct((nf, nz, nx), jnp.float32)
     zface = jax.ShapeDtypeStruct((nf, ny, nx), jnp.float32)
-    outs = [full] + ([yface, yface, zface, zface] if with_faces else [])
+    packed = jax.ShapeDtypeStruct((len(upper_blocks(nx)) * STEP, STEP), jnp.float32)
+    outs = [full] + ([yface, yface, zface, zface] if with_faces else [packed])
     return pl.pallas_call(
-        functools.partial(relax_kernel, with_faces),
+        functools.partial(relax_kernel, with_faces, total_rows),
         out_shape=outs,
         in_specs=[pl.BlockSpec(memory_space=pltpu.VMEM)] * 10,
         out_specs=[pl.BlockSpec(memory_space=pltpu.VMEM)] * len(outs),
         scratch_shapes=[
             pltpu.VMEM((nf, ny + 2, nz + 16, nx), jnp.float32),
             pltpu.VMEM((ny + 2, nz + 16, nx), jnp.float32),
-        ],
+        ]
+        + ([] if with_faces else [pltpu.VMEM((nx, nx), jnp.float32)] * 2),
         compiler_params=pltpu.CompilerParams(vmem_limit_bytes=VMEM_LIMIT),
         name="relax",
     )(u, k, *faces, *kfaces)
+
+
+def tree_sum(terms):
+    while len(terms) > 1:
+        terms = [a + b for a, b in zip(terms[::2], terms[1::2])]
+    return terms[0]
 
 
 def eliminate(block):
@@ -110,27 +150,33 @@
     lane8 = lax.broadcasted_iota(jnp.int32, (8, size), 1)
     work = [block[8 * g : 8 * g + 8] for g in range(groups)]
     side = [jnp.where(row8 + 8 * g == lane8, 1.0, 0.0) for g in range(groups)]
-    for j in range(size):
-        g, r = divmod(j, 8)
-        spread = jnp.broadcast_to(work[g][:, j : j + 1], (8, size))
-        inv = 1.0 / jnp.broadcast_to(spread[r : r + 1], (8, size))
-        row = jnp.broadcast_to(work[g][r : r + 1], (8, size)) * inv
-        arow = jnp.broadcast_to(side[g][r : r + 1], (8, size)) * inv
-        for q in range(g, groups):
-            if q == g:
-                if r == 7:
-                    continue
-                mult = jnp.where(row8 > r, spread, 0.0)
-            else:
-                mult = jnp.broadcast_to(work[q][:, j : j + 1], (8, size))
-            work[q] = work[q] - mult * row
-            side[q] = side[q] - mult * arow
+    for p in range(groups):
+        rows, arows = work[p], side[p]
+        spread = [jnp.broadcast_to(rows[:, 8 * p + m : 8 * p + m + 1], (8, size)) for m in range(8)]
+        unit, aunit = [], []
+        for m in range(8):
+            inv = 1.0 / jnp.broadcast_to(spread[m][m : m + 1], (8, size))
+            unit.append(jnp.broadcast_to(rows[m : m + 1], (8, size)) * inv)
+            aunit.append(jnp.broadcast_to(arows[m : m + 1], (8, size)) * inv)
+            if m < 7:
+                mult = jnp.where(row8 > m, spread[m], 0.0)
+                rows = rows - mult * unit[m]
+                arows = arows - mult * aunit[m]
+                for t in range(m + 1, 8):
+                    spread[t] = spread[t] - mult * (jnp.broadcast_to(spread[t][m : m + 1], (8, size)) * inv)
+        work[p], side[p] = rows, arows
+        if p + 1 < groups:
+            tall = rows.T
+            for q in range(p + 1, groups):
+                mults = [jnp.broadcast_to(tall[8 * q : 8 * q + 8, m : m + 1], (8, size)) for m in range(8)]
+                work[q] = work[q] - tree_sum([a * b for a, b in zip(mults, unit)])
+                side[q] = side[q] - tree_sum([a * b for a, b in zip(mults, aunit)])
     return jnp.concatenate(work, axis=0), jnp.concatenate(side, axis=0)
 
 
 def factor_kernel(gram_ref, factor_ref, inv_ref, work, side):
-    n = gram_ref.shape[0]
-    step = min(n, STEP)
+    n = factor_ref.shape[0]
+    step = STEP
     count = n // step
     big = (((1,), (0,)), ((), ()))
     tall = (((0,), (0,)), ((), ()))
@@ -138,7 +184,9 @@
     cols = lax.broadcasted_iota(jnp.int32, (step, step), 1)
     col_n = lax.broadcasted_iota(jnp.int32, (step, n), 1)
     row_n = lax.broadcasted_iota(jnp.int32, (step, n), 0)
-    work[...] = gram_ref[...]
+    work[...] = jnp.zeros_like(work)
+    for b, (i, j) in enumerate(upper_blocks(n)):
+        work[i * step : (i + 1) * step, j * step : (j + 1) * step] = gram_ref[b * step : (b + 1) * step, :]
     side[...] = jnp.zeros_like(side)
 
     def block_step(k, carry):
@@ -169,17 +217,105 @@
     lax.fori_loop(0, count, block_step, 0)
 
 
-def factor_call(gram):
-    shape = jax.ShapeDtypeStruct(gram.shape, jnp.float32)
+def factor_call(gram, n):
+    shape = jax.ShapeDtypeStruct((n, n), jnp.float32)
     return pl.pallas_call(
         factor_kernel,
         out_shape=[shape, shape],
         in_specs=[pl.BlockSpec(memory_space=pltpu.VMEM)],
         out_specs=[pl.BlockSpec(memory_space=pltpu.VMEM)] * 2,
-        scratch_shapes=[pltpu.VMEM(gram.shape, jnp.float32)] * 2,
+        scratch_shapes=[pltpu.VMEM((n, n), jnp.float32)] * 2,
         compiler_params=pltpu.CompilerParams(vmem_limit_bytes=VMEM_LIMIT),
         name="factor",
     )(gram)
+
+
+FAST = 2
+
+
+def sum_kernel(nby, nbz, in_ref, out_ref, land_a, land_b, part, send_a, recv_a, send_b, recv_b, send_c, recv_c, send_d, recv_d):
+    na, nb = nby * FAST, nbz // FAST
+    rows_a = in_ref.shape[0] // na
+    rows_b = rows_a // nb
+    by, bz = lax.axis_index("by"), lax.axis_index("bz")
+    a = by * FAST + bz % FAST
+    z = bz // FAST
+
+    def plane_peer(d):
+        t = (a + d) % na
+        return t, (t // FAST, z * FAST + t % FAST)
+
+    def line_peer(d):
+        t = (z + d) % nb
+        return t, (by, t * FAST + bz % FAST)
+
+    barrier = pltpu.get_barrier_semaphore()
+    for d in range(1, na):
+        pl.semaphore_signal(barrier, inc=1, device_id=plane_peer(d)[1], device_id_type=pl.DeviceIdType.MESH)
+    for d in range(1, nb):
+        pl.semaphore_signal(barrier, inc=1, device_id=line_peer(d)[1], device_id_type=pl.DeviceIdType.MESH)
+    pl.semaphore_wait(barrier, na + nb - 2)
+
+    def exchange(peer, count, send, recv, source, target):
+        copies = []
+        for d in range(1, count):
+            t, where = peer(d)
+            copy = pltpu.make_async_remote_copy(
+                src_ref=source(t),
+                dst_ref=target(d),
+                send_sem=send.at[d - 1],
+                recv_sem=recv.at[d - 1],
+                device_id=where,
+                device_id_type=pl.DeviceIdType.MESH,
+            )
+            copy.start()
+            copies.append(copy)
+        for copy in copies:
+            copy.wait()
+
+    def rows_at(base, size):
+        return pl.ds(pl.multiple_of(base, 8), size)
+
+    exchange(plane_peer, na, send_a, recv_a, lambda t: in_ref.at[rows_at(t * rows_a, rows_a)], lambda d: land_a.at[d - 1])
+    part[...] = in_ref[rows_at(a * rows_a, rows_a), :] + tree_any([land_a[d] for d in range(na - 1)])
+    exchange(line_peer, nb, send_b, recv_b, lambda t: part.at[rows_at(t * rows_b, rows_b)], lambda d: land_b.at[d - 1])
+    mine = rows_at(a * rows_a + z * rows_b, rows_b)
+    out_ref[mine, :] = part[rows_at(z * rows_b, rows_b), :] + tree_any([land_b[d] for d in range(nb - 1)])
+    exchange(line_peer, nb, send_c, recv_c, lambda t: out_ref.at[mine], lambda d: out_ref.at[mine])
+    ours = rows_at(a * rows_a, rows_a)
+    exchange(plane_peer, na, send_d, recv_d, lambda t: out_ref.at[ours], lambda d: out_ref.at[ours])
+
+
+def tree_any(terms):
+    total = terms[0]
+    for term in terms[1:]:
+        total = total + term
+    return total
+
+
+def sum_call(packed):
+    nby, nbz = lax.axis_size("by"), lax.axis_size("bz")
+    na, nb = nby * FAST, nbz // FAST
+    rows, cols = packed.shape
+    if nbz % FAST or nb < 2 or rows % (8 * na * nb):
+        return lax.psum(packed, ("by", "bz"))
+    rows_a = rows // na
+    rows_b = rows_a // nb
+    sems = [pltpu.SemaphoreType.DMA((c - 1,)) for c in (na, na, nb, nb, nb, nb, na, na)]
+    return pl.pallas_call(
+        functools.partial(sum_kernel, nby, nbz),
+        out_shape=jax.ShapeDtypeStruct(packed.shape, jnp.float32),
+        in_specs=[pl.BlockSpec(memory_space=pltpu.VMEM)],
+        out_specs=pl.BlockSpec(memory_space=pltpu.VMEM),
+        scratch_shapes=[
+            pltpu.VMEM((na - 1, rows_a, cols), jnp.float32),
+            pltpu.VMEM((nb - 1, rows_b, cols), jnp.float32),
+            pltpu.VMEM((rows_a, cols), jnp.float32),
+            *sems,
+        ],
+        compiler_params=pltpu.CompilerParams(collective_id=0, has_side_effects=True, vmem_limit_bytes=VMEM_LIMIT),
+        name="sum_all",
+    )(packed)
 
 
 def on_device(fields, conductance):
@@ -196,13 +332,9 @@
     kfaces = [a[nf] for a in (*yfaces, *zfaces)]
     once, ylo, yhi, zlo, zhi = relax_call(fields, conductance, faces, kfaces, True)
     again = (*shift_faces((ylo, yhi), "by"), *shift_faces((zlo, zhi), "bz"))
-    relaxed = relax_call(once, conductance, again, kfaces, False)[0]
+    relaxed, packed = relax_call(once, conductance, again, kfaces, False, total_rows)
     rows = relaxed.reshape(-1, nx)
-    gram = lax.dot_general(
-        rows, rows, (((0,), (0,)), ((), ())), precision=HIGH, preferred_element_type=jnp.float32
-    )
-    gram = lax.psum(gram / jnp.float32(total_rows), ("by", "bz"))
-    factor, linv = factor_call(gram)
+    factor, linv = factor_call(sum_call(packed), nx)
     basis = lax.dot_general(
         rows, linv, (((1,), (1,)), ((), ())), precision=HIGH, preferred_element_type=jnp.float32
     )

time: 337 us -> 165 us (0.49)
  waiting for transfers between devices: 149 us -> 16.1 us
  matrix products: 30.4 us -> 11.4 us
  between operations: 14.2 us -> 0.81 us
  Pallas kernels: 109 us -> 103 us
    psum x1 -> x0, waiting for transfers between devices: 133 us -> none  [on_device(): gram = lax.psum(gram / jnp.float32(total_rows), ('by', 'bz'))]
    pallas_call x1, Pallas kernels: 77.3 us -> 32.6 us  [factor_call(): pl.pallas_call(factor_kernel, out_shape=[shape, shape], in_specs=[pl.Bloc...]
    pallas_call x2 -> x3, Pallas kernels: 32.1 us -> 70.6 us  [the longest x2 37.7 us: relax_call(): pl.pallas_call(functools.partial(relax_kernel, with_faces, total_rows), o...]
    dot_general x1 -> x0, matrix products: 19 us -> none  [on_device(): lax.dot_general(rows, rows, (((0,), (0,)), ((), ())), precision=HIGH, pre...]
  transfers between devices with their start and end apart: 9 -> 8, of which waited for: 4 -> 3; matrix products, arithmetic and copies ran while one was open for 2% -> 4% of each run, Pallas kernels for 0% -> 0%
where the time goes in v2:
time: 165 us
  Pallas kernels  103 us (62%)
  starting transfers between devices  19.9 us (12%)
  waiting for transfers between devices  16.1 us (10%)
  local copies, waits for them, and re-layouts  12.8 us (8%)
  matrix products  11.4 us (7%)
    pallas_call x2, Pallas kernels, relax_call(): pl.pallas_call(functools.partial(relax_kernel, with_faces, total_rows), o...  37.7 us
    pallas_call x1, Pallas kernels, sum_call(): pl.pallas_call(functools.partial(sum_kernel, nby, nbz), out_shape=jax.Sha...  33 us
    pallas_call x1, Pallas kernels, factor_call(): pl.pallas_call(factor_kernel, out_shape=[shape, shape], in_specs=[pl.Bloc...  32.6 us
    ppermute x4, starting transfers between devices, shift_faces(): below = lax.ppermute(tail, axis, [(i, i + 1) for i in range(count - 1)])  14.5 us
    dot_general x1, matrix products, on_device(): lax.dot_general(rows, linv, (((1,), (1,)), ((), ())), precision=HIGH, pre...  11.4 us
    ppermute x4, waiting for transfers between devices, shift_faces(): below = lax.ppermute(tail, axis, [(i, i + 1) for i in range(count - 1)])  11.3 us
    ppermute x4, starting transfers between devices, shift_faces(): above = lax.ppermute(head, axis, [(i + 1, i) for i in range(count - 1)])  5.35 us
    ppermute x4, waiting for transfers between devices, shift_faces(): above = lax.ppermute(head, axis, [(i + 1, i) for i in range(count - 1)])  4.84 us
  transfers between devices with their start and end apart: 8, of which 3 were waited for; matrix products, arithmetic and copies ran while one was open for 4% of the time, Pallas kernels for 0%

profile of v2, /device:TPU:0, one launch (start us, length us, event | category | flops | bytes accessed | tf_op | source)
XLA Modules:
  0.0 164.5 jit_solution(13232347385966891307)
XLA Ops:
  0.6 1.1 fusion.3
  1.7 2.8 %fusion.2 = (f32[8,16,1,512]{3,2,1,0:T(1,128)S(1)}, f32[8,16,1,512]{3,2,1,0:T(1,128)S(1)}) fusion(f32[8,16,32,512]{3,2,1,0:T(8,128)} %u_ref.1), kind=kLoop, calls=%fused_computation.16 | loop fusion | bytes 1048576 | tf_op jit(solution)/shard_map/slice | solution.py:329
  4.6 4.9 %collective-permute-start.2 = (f32[9,16,512]{2,1,0:T(8,128)S(1)}, f32[9,16,512]{2,1,0:T(8,128)S(1)}, u32[]{:S(2)}, u32[]{:S(2)}) collective-permute-start(f32[9,16,512]{2,1,0:T(8,128)S(1)} %pad_maximum_fusion.2), channel_id=1, source_target_pairs={{0,1},{1,2},{2,3},{3,4},{4,5},{5,6},{6,7},{8,9},{9,10},{10,11},{11... | collective-permute-start | bytes 884744 | tf_op jit(solution)/shard_map/ppermute | solution.py:19
  9.5 1.3 collective-permute-start.3
  10.8 1.3 slice_bitcast_fusion
  12.1 0.9 fusion.4
  13.0 1.5 collective-permute-start
  14.6 1.3 collective-permute-start.1
  15.9 6.1 %collective-permute-done.2 = f32[9,16,512]{2,1,0:T(8,128)S(1)} collective-permute-done((f32[9,16,512]{2,1,0:T(8,128)S(1)}, f32[9,16,512]{2,1,0:T(8,128)S(1)}, u32[]{:S(2)}, u32[]{:S(2)}) %collective-permute-start.2) | collective-permute-done | bytes 294944 | tf_op jit(solution)/shard_map/ppermute | solution.py:19
  22.0 0.7 slice.66.zb_ref
  22.7 0.0 collective-permute-done.3
  22.7 0.7 slice.67.za_ref
  23.4 0.6 slice_bitcast_fusion.5.kzb_ref
  24.0 0.6 slice_bitcast_fusion.4.kza_ref
  24.7 0.0 collective-permute-done
  24.7 0.8 slice.64.yb_ref
  25.5 0.6 slice_bitcast_fusion.3.kyb_ref
  26.1 0.0 collective-permute-done.1
  26.1 0.6 slice_bitcast_fusion.2.kya_ref
  26.8 0.9 slice.65.ya_ref
  27.6 16.4 %relax.2 = (f32[8,16,32,512]{3,2,1,0:T(8,128)}, f32[8,32,512]{2,1,0:T(8,128)}, f32[8,32,512]{2,1,0:T(8,128)}, f32[8,16,512]{2,1,0:T(8,128)}, f32[8,16,512]{2,1,0:T(8,128)}) custom-call(f32[8,16,32,512]{3,2,1,0:T(8,128)} %u_ref.1, f32[16,32,512]{2,1,0:T(8,128)} %k_ref.3, f32[8,32,512]{2,1,0:T(8,128)} %slice.64.yb_ref, f32[8,32,512]{2,1,0:T(8,128)} %slice.65.ya_ref, ...), custom_call_target="tpu_custom_call" | custom-call | tf_op jit(solution)/shard_map/relax/pallas_call | solution.py:125
  44.0 3.6 %collective-permute-start.4 = (f32[8,32,512]{2,1,0:T(8,128)}, f32[8,32,512]{2,1,0:T(8,128)S(1)}, u32[]{:S(2)}, u32[]{:S(2)}) collective-permute-start(f32[8,32,512]{2,1,0:T(8,128)} %get-tuple-element.12), channel_id=1, source_target_pairs={{0,8},{8,16},{16,24},{1,9},{9,17},{17,25},{2,10},{10,18},{18,26},{... | collective-permute-start | bytes 1572872 | tf_op jit(solution)/shard_map/ppermute | solution.py:19
  47.7 1.3 collective-permute-start.5
  49.0 4.6 %collective-permute-start.6 = (f32[8,16,512]{2,1,0:T(8,128)}, f32[8,16,512]{2,1,0:T(8,128)S(1)}, u32[]{:S(2)}, u32[]{:S(2)}) collective-permute-start(f32[8,16,512]{2,1,0:T(8,128)} %get-tuple-element.14), channel_id=1, source_target_pairs={{0,1},{1,2},{2,3},{3,4},{4,5},{5,6},{6,7},{8,9},{9,10},{10,11},{11... | collective-permute-start | bytes 786440 | tf_op jit(solution)/shard_map/ppermute | solution.py:19
  53.5 1.5 collective-permute-start.7
  55.0 5.2 %collective-permute-done.6.zb_ref = f32[8,16,512]{2,1,0:T(8,128)S(1)} collective-permute-done((f32[8,16,512]{2,1,0:T(8,128)}, f32[8,16,512]{2,1,0:T(8,128)S(1)}, u32[]{:S(2)}, u32[]{:S(2)}) %collective-permute-start.6) | collective-permute-done | bytes 262176 | tf_op jit(solution)/shard_map/ppermute | solution.py:19
  60.2 0.0 copy-start.2
  60.2 4.8 %collective-permute-done.7.za_ref = f32[8,16,512]{2,1,0:T(8,128)S(1)} collective-permute-done((f32[8,16,512]{2,1,0:T(8,128)}, f32[8,16,512]{2,1,0:T(8,128)S(1)}, u32[]{:S(2)}, u32[]{:S(2)}) %collective-permute-start.7) | collective-permute-done | bytes 262176 | tf_op jit(solution)/shard_map/ppermute | solution.py:20
  65.1 0.0 copy-start.3
  65.1 0.0 collective-permute-done.4.yb_ref
  65.1 0.0 copy-start
  65.1 0.0 collective-permute-done.5.ya_ref
  65.1 0.0 copy-start.1
  65.1 0.0 copy-done.2
  65.1 0.7 copy-done.3
  65.8 0.2 copy-done
  66.0 0.2 copy-done.1
  66.2 21.3 %relax.3 = (f32[8,16,32,512]{3,2,1,0:T(8,128)}, f32[1280,128]{1,0:T(8,128)}) custom-call(f32[8,16,32,512]{3,2,1,0:T(8,128)} %get-tuple-element.11.u_ref, f32[16,32,512]{2,1,0:T(8,128)} %k_ref.3, f32[8,32,512]{2,1,0:T(8,128)} %copy-done, f32[8,32,512]{2,1,0:T(8,128)} %copy-done.1, f32[8,16,512]{2,1,0:T(8,128)} %copy-done.2, f32[8,16,512]{2,1,0:T(8,128)} %copy-done.3, ...), custom_call_target="tpu_custom_call" | custom-call | tf_op jit(solution)/shard_map/relax/pallas_call | solution.py:125
  87.5 33.0 %sum_all.1.gram_ref = f32[1280,128]{1,0:T(8,128)} custom-call(f32[1280,128]{1,0:T(8,128)} %get-tuple-element.17.in_ref), custom_call_target="tpu_custom_call" | custom-call | tf_op jit(solution)/shard_map/sum_all/pallas_call | solution.py:305
  120.5 32.6 %factor.1 = (f32[512,512]{1,0:T(8,128)}, f32[512,512]{1,0:T(8,128)}) custom-call(f32[1280,128]{1,0:T(8,128)} %sum_all.1.gram_ref), custom_call_target="tpu_custom_call" | custom-call | tf_op jit(solution)/shard_map/factor/pallas_call | solution.py:222
  153.1 11.4 %fusion = f32[8,16,32,512]{3,2,1,0:T(8,128)} fusion(f32[8,16,32,512]{3,2,1,0:T(8,128)} %get-tuple-element.16, f32[512,512]{1,0:T(8,128)} %get-tuple-element.18), kind=kOutput, calls=%fused_computation | convolution fusion | flops 6442450944 | bytes 17825792 | tf_op jit(solution)/shard_map/dot_general | solution.py:338
  (8 shorter events, 0.2 us)
Async XLA Ops:
  4.6 17.4 %collective-permute-start.2 = (f32[9,16,512]{2,1,0:T(8,128)S(1)}, f32[9,16,512]{2,1,0:T(8,128)S(1)}, u32[]{:S(2)}, u32[]{:S(2)}) collective-permute-start(f32[9,16,512]{2,1,0:T(8,128)S(1)} %pad_maximum_fusion.2), channel_id=1, source_target_pairs={{0,1},{1,2},{2,3},{3,4},{4,5},{5,6},{6,7},{8,9},{9,10},{10,11},{11... | collective-permute-start | bytes 884744 | tf_op jit(solution)/shard_map/ppermute | solution.py:19
  9.5 13.2 %collective-permute-start.3 = (f32[9,16,512]{2,1,0:T(8,128)S(1)}, f32[9,16,512]{2,1,0:T(8,128)S(1)}, u32[]{:S(2)}, u32[]{:S(2)}) collective-permute-start(f32[9,16,512]{2,1,0:T(8,128)S(1)} %pad_maximum_fusion.3), channel_id=1, source_target_pairs={{1,0},{2,1},{3,2},{4,3},{5,4},{6,5},{7,6},{9,8},{10,9},{11,10},{12... | collective-permute-start | bytes 884744 | tf_op jit(solution)/shard_map/ppermute | solution.py:20
  13.0 11.6 %collective-permute-start = (f32[9,32,512]{2,1,0:T(8,128)S(1)}, f32[9,32,512]{2,1,0:T(8,128)S(1)}, u32[]{:S(2)}, u32[]{:S(2)}) collective-permute-start(f32[9,32,512]{2,1,0:T(8,128)S(1)} %pad_maximum_fusion), channel_id=1, source_target_pairs={{0,8},{8,16},{16,24},{1,9},{9,17},{17,25},{2,10},{10,18},{18,26},{... | collective-permute-start | bytes 1769480 | tf_op jit(solution)/shard_map/ppermute | solution.py:19
  14.6 11.5 %collective-permute-start.1 = (f32[9,32,512]{2,1,0:T(8,128)S(1)}, f32[9,32,512]{2,1,0:T(8,128)S(1)}, u32[]{:S(2)}, u32[]{:S(2)}) collective-permute-start(f32[9,32,512]{2,1,0:T(8,128)S(1)} %pad_maximum_fusion.1), channel_id=1, source_target_pairs={{8,0},{16,8},{24,16},{9,1},{17,9},{25,17},{10,2},{18,10},{26,18},{... | collective-permute-start | bytes 1769480 | tf_op jit(solution)/shard_map/ppermute | solution.py:20
  44.0 21.0 %collective-permute-start.4 = (f32[8,32,512]{2,1,0:T(8,128)}, f32[8,32,512]{2,1,0:T(8,128)S(1)}, u32[]{:S(2)}, u32[]{:S(2)}) collective-permute-start(f32[8,32,512]{2,1,0:T(8,128)} %get-tuple-element.12), channel_id=1, source_target_pairs={{0,8},{8,16},{16,24},{1,9},{9,17},{17,25},{2,10},{10,18},{18,26},{... | collective-permute-start | bytes 1572872 | tf_op jit(solution)/shard_map/ppermute | solution.py:19
  47.7 17.4 %collective-permute-start.5 = (f32[8,32,512]{2,1,0:T(8,128)}, f32[8,32,512]{2,1,0:T(8,128)S(1)}, u32[]{:S(2)}, u32[]{:S(2)}) collective-permute-start(f32[8,32,512]{2,1,0:T(8,128)} %get-tuple-element.13), channel_id=1, source_target_pairs={{8,0},{16,8},{24,16},{9,1},{17,9},{25,17},{10,2},{18,10},{26,18},{... | collective-permute-start | bytes 1572872 | tf_op jit(solution)/shard_map/ppermute | solution.py:20
  49.0 11.3 %collective-permute-start.6 = (f32[8,16,512]{2,1,0:T(8,128)}, f32[8,16,512]{2,1,0:T(8,128)S(1)}, u32[]{:S(2)}, u32[]{:S(2)}) collective-permute-start(f32[8,16,512]{2,1,0:T(8,128)} %get-tuple-element.14), channel_id=1, source_target_pairs={{0,1},{1,2},{2,3},{3,4},{4,5},{5,6},{6,7},{8,9},{9,10},{10,11},{11... | collective-permute-start | bytes 786440 | tf_op jit(solution)/shard_map/ppermute | solution.py:19
  53.5 11.5 %collective-permute-start.7 = (f32[8,16,512]{2,1,0:T(8,128)}, f32[8,16,512]{2,1,0:T(8,128)S(1)}, u32[]{:S(2)}, u32[]{:S(2)}) collective-permute-start(f32[8,16,512]{2,1,0:T(8,128)} %get-tuple-element.15), channel_id=1, source_target_pairs={{1,0},{2,1},{3,2},{4,3},{5,4},{6,5},{7,6},{9,8},{10,9},{11,10},{12... | collective-permute-start | bytes 786440 | tf_op jit(solution)/shard_map/ppermute | solution.py:20
  60.2 4.9 %copy-start.2 = (f32[8,16,512]{2,1,0:T(8,128)}, f32[8,16,512]{2,1,0:T(8,128)S(1)}, u32[]{:S(2)}) copy-start(f32[8,16,512]{2,1,0:T(8,128)S(1)} %collective-permute-done.6.zb_ref) | copy-start | bytes 786436
  65.1 0.7 copy-start.3
  65.1 0.9 copy-start
  65.1 1.1 copy-start.1

commit v3 on v2

--- a/solution.py
+++ b/solution.py
@@ -13,128 +13,234 @@
 STEP = 128
 
 
-def shift_faces(cells, axis):
-    count = lax.axis_size(axis)
-    head, tail = cells
-    below = lax.ppermute(tail, axis, [(i, i + 1) for i in range(count - 1)])
-    above = lax.ppermute(head, axis, [(i + 1, i) for i in range(count - 1)])
-    return below, above
-
-
 def upper_blocks(n):
     count = n // STEP
     return [(i, j) for i in range(count) for j in range(i, count)]
 
 
-def relax_kernel(with_faces, total_rows, u_ref, k_ref, yb_ref, ya_ref, zb_ref, za_ref, kyb_ref, kya_ref, kzb_ref, kza_ref, *rest):
-    if with_faces:
-        out_ref, ylo_ref, yhi_ref, zlo_ref, zhi_ref, ext, root = rest
-    else:
-        out_ref, gram_ref, ext, root, head, cross = rest
+def strip(src, root, store, y, z, nf, nx, lane):
+    plain = root[y + 1, pl.ds(8 + z, 8), :]
+    centre = 0.125 * plain
+    wyp = centre * root[y + 2, pl.ds(8 + z, 8), :]
+    wym = centre * root[y, pl.ds(8 + z, 8), :]
+    wzp = centre * root[y + 1, pl.ds(9 + z, 8), :]
+    wzm = centre * root[y + 1, pl.ds(7 + z, 8), :]
+    wxp = jnp.where(lane == nx - 1, 0.0, centre * pltpu.roll(plain, nx - 1, 1))
+    wxm = jnp.where(lane == 0, 0.0, centre * pltpu.roll(plain, 1, 1))
+    keep = 1.0 - (((wyp + wym) + (wzp + wzm)) + (wxp + wxm))
+    for f in range(nf):
+        mid = src[f, y + 1, pl.ds(8 + z, 8), :]
+        near = wyp * src[f, y + 2, pl.ds(8 + z, 8), :] + wym * src[f, y, pl.ds(8 + z, 8), :]
+        side = wzp * src[f, y + 1, pl.ds(9 + z, 8), :] + wzm * src[f, y + 1, pl.ds(7 + z, 8), :]
+        along = wxp * pltpu.roll(mid, nx - 1, 1) + wxm * pltpu.roll(mid, 1, 1)
+        store(f, y, z, (keep * mid + near) + (side + along))
+
+
+def relax_kernel(nby, nbz, u_ref, k_ref, out_ref, ext, again, root, kland, zsend, zland, zsend2, zland2, load_sem, send, recv):
     nf, ny, nz, nx = u_ref.shape
     top = 8 + nz
+    by, bz = lax.axis_index("by"), lax.axis_index("bz")
+    has = [by > 0, by < nby - 1, bz > 0, bz < nbz - 1]
+    peer = [(by - 1, bz), (by + 1, bz), (by, bz - 1), (by, bz + 1)]
+    inner = pl.ds(8, nz)
+    halo = [0, ny + 1]
+    mesh_id = pl.DeviceIdType.MESH
+
+    load = pltpu.make_async_copy(u_ref, ext.at[:, pl.ds(1, ny), inner, :], load_sem)
+    load.start()
+
+    def send_item(d, base, src, place):
+        return pltpu.make_async_remote_copy(
+            src_ref=src,
+            dst_ref=place((d + 1) % 2),
+            send_sem=send.at[base + d % 2],
+            recv_sem=recv.at[base + (d + 1) % 2],
+            device_id=peer[d],
+            device_id_type=mesh_id,
+        )
+
+    def recv_item(d, base, src, place):
+        return pltpu.make_async_remote_copy(
+            src_ref=src,
+            dst_ref=place(d % 2),
+            send_sem=send.at[base + d % 2],
+            recv_sem=recv.at[base + d % 2],
+            device_id=peer[d],
+            device_id_type=mesh_id,
+        )
+
+    def start(items):
+        for d, base, src, place in items:
+            @pl.when(has[d])
+            def _(d=d, base=base, src=src, place=place):
+                send_item(d, base, src, place).start()
+
+    def finish(items):
+        for d, base, src, place in items:
+            @pl.when(has[d])
+            def _(d=d, base=base, src=src, place=place):
+                recv_item(d, base, src, place).wait_recv()
+                send_item(d, base, src, place).wait_send()
+
+    barrier = pltpu.get_barrier_semaphore()
+    for d in range(4):
+        @pl.when(has[d])
+        def _(d=d):
+            pl.semaphore_signal(barrier, inc=1, device_id=peer[d], device_id_type=mesh_id)
+    pl.semaphore_wait(barrier, sum(jnp.where(h, 1, 0) for h in has))
+
+    ends = [0, ny - 1]
+    first_y = [(d, 0, u_ref.at[:, ends[d]], lambda s: ext.at[:, halo[s], inner, :]) for d in range(2)]
+    first_k = [(d, 2, k_ref.at[ends[d]], lambda s: kland.at[s]) for d in range(2)]
+    start(first_y + first_k)
+
+    for d in range(2):
+        @pl.when(jnp.logical_not(has[d]))
+        def _(d=d):
+            for f in range(nf):
+                ext[f, halo[d], inner, :] = jnp.zeros((nz, nx), jnp.float32)
+                again[f, halo[d], inner, :] = jnp.zeros((nz, nx), jnp.float32)
+            kland[d] = jnp.zeros((nz, nx), jnp.float32)
+
+        @pl.when(jnp.logical_not(has[d + 2]))
+        def _(d=d):
+            zland[d] = jnp.zeros(zland.shape[1:], jnp.float32)
+            zland2[d] = jnp.zeros(zland2.shape[1:], jnp.float32)
+
+    zsend[0, nf] = k_ref[:, 0, :]
+    zsend[1, nf] = k_ref[:, nz - 1, :]
+    load.wait()
+    for f in range(nf):
+        zsend[0, f] = ext[f, pl.ds(1, ny), 8, :]
+        zsend[1, f] = ext[f, pl.ds(1, ny), top - 1, :]
+    first_z = [(d, 4, zsend.at[d - 2], lambda s: zland.at[s]) for d in (2, 3)]
+    start(first_z)
 
     def fill_root(y, carry):
-        root[y + 1, pl.ds(8, nz), :] = jnp.sqrt(k_ref[y])
+        root[y + 1, inner, :] = jnp.sqrt(k_ref[y])
         return carry
 
     lax.fori_loop(0, ny, fill_root, 0)
-    root[0, pl.ds(8, nz), :] = jnp.sqrt(kyb_ref[...])
-    root[ny + 1, pl.ds(8, nz), :] = jnp.sqrt(kya_ref[...])
-    root[pl.ds(1, ny), 7:8, :] = jnp.sqrt(kzb_ref[...])[:, None, :]
-    root[pl.ds(1, ny), top : top + 1, :] = jnp.sqrt(kza_ref[...])[:, None, :]
-
-    def fill(f, carry):
-        def fill_y(y, c):
-            ext[f, y + 1, pl.ds(8, nz), :] = u_ref[f, y]
-            return c
-
-        lax.fori_loop(0, ny, fill_y, 0)
-        ext[f, 0, pl.ds(8, nz), :] = yb_ref[f]
-        ext[f, ny + 1, pl.ds(8, nz), :] = ya_ref[f]
-        ext[f, pl.ds(1, ny), 7:8, :] = zb_ref[f][:, None, :]
-        ext[f, pl.ds(1, ny), top : top + 1, :] = za_ref[f][:, None, :]
-        return carry
-
-    lax.fori_loop(0, nf, fill, 0)
-
     lane = lax.broadcasted_iota(jnp.int32, (8, nx), 1)
 
-    def plane(y, carry):
-        for z in range(0, nz, 8):
-            centre = 0.125 * root[y + 1, pl.ds(8 + z, 8), :]
-            plain = root[y + 1, pl.ds(8 + z, 8), :]
-            wyp = centre * root[y + 2, pl.ds(8 + z, 8), :]
-            wym = centre * root[y, pl.ds(8 + z, 8), :]
-            wzp = centre * root[y + 1, pl.ds(9 + z, 8), :]
-            wzm = centre * root[y + 1, pl.ds(7 + z, 8), :]
-            wxp = jnp.where(lane == nx - 1, 0.0, centre * pltpu.roll(plain, nx - 1, 1))
-            wxm = jnp.where(lane == 0, 0.0, centre * pltpu.roll(plain, 1, 1))
-            keep = 1.0 - (((wyp + wym) + (wzp + wzm)) + (wxp + wxm))
-            for f in range(nf):
-                mid = ext[f, y + 1, pl.ds(8 + z, 8), :]
-                near = wyp * ext[f, y + 2, pl.ds(8 + z, 8), :] + wym * ext[f, y, pl.ds(8 + z, 8), :]
-                side = wzp * ext[f, y + 1, pl.ds(9 + z, 8), :] + wzm * ext[f, y + 1, pl.ds(7 + z, 8), :]
-                along = wxp * pltpu.roll(mid, nx - 1, 1) + wxm * pltpu.roll(mid, 1, 1)
-                out_ref[f, y, pl.ds(z, 8), :] = (keep * mid + near) + (side + along)
-        return carry
-
-    lax.fori_loop(0, ny, plane, 0)
-    if with_faces:
+    def to_again(f, y, z, value):
+        again[f, y + 1, pl.ds(8 + z, 8), :] = value
+
+    def to_out(f, y, z, value):
+        out_ref[f, y, pl.ds(z, 8), :] = value
+
+    def inside(src, store):
+        def body(y, carry):
+            for z in range(8, nz - 8, 8):
+                strip(src, root, store, y, z, nf, nx, lane)
+            return carry
+
+        lax.fori_loop(1, ny - 1, body, 0)
+
+    def border(src, store):
+        def planes(i, carry):
+            for z in range(0, nz, 8):
+                strip(src, root, store, i * (ny - 1), z, nf, nx, lane)
+            return carry
+
+        def strips(y, carry):
+            for z in (0, nz - 8):
+                strip(src, root, store, y, z, nf, nx, lane)
+            return carry
+
+        lax.fori_loop(0, 2, planes, 0)
+        lax.fori_loop(1, ny - 1, strips, 0)
+
+    inside(ext, to_again)
+    finish(first_y + first_k + first_z)
+    for d, row in ((0, 7), (1, top)):
+        root[halo[d], inner, :] = jnp.sqrt(kland[d])
+        root[pl.ds(1, ny), row : row + 1, :] = jnp.sqrt(zland[d, nf])[:, None, :]
         for f in range(nf):
-            ylo_ref[f] = out_ref[f, 0]
-            yhi_ref[f] = out_ref[f, ny - 1]
-            zlo_ref[f] = out_ref[f, :, 0, :]
-            zhi_ref[f] = out_ref[f, :, nz - 1, :]
-    else:
-        pack_gram(total_rows, out_ref, gram_ref, head, cross)
-
-
-def pack_gram(total_rows, rows_ref, gram_ref, head, cross):
-    nf, ny, nz, nx = rows_ref.shape
+            ext[f, pl.ds(1, ny), row : row + 1, :] = zland[d, f][:, None, :]
+    border(ext, to_again)
+
+    for f in range(nf):
+        zsend2[0, f] = again[f, pl.ds(1, ny), 8, :]
+        zsend2[1, f] = again[f, pl.ds(1, ny), top - 1, :]
+    second = [(d, 6, again.at[:, ends[d] + 1, inner, :], lambda s: again.at[:, halo[s], inner, :]) for d in range(2)]
+    second += [(d, 8, zsend2.at[d - 2], lambda s: zland2.at[s]) for d in (2, 3)]
+    start(second)
+    inside(again, to_out)
+    finish(second)
+    for d, row in ((0, 7), (1, top)):
+        for f in range(nf):
+            again[f, pl.ds(1, ny), row : row + 1, :] = zland2[d, f][:, None, :]
+    border(again, to_out)
+
+
+def relax_call(u, k):
+    nf, ny, nz, nx = u.shape
+    cells = pltpu.VMEM((nf, ny + 2, nz + 16, nx), jnp.float32)
+    return pl.pallas_call(
+        functools.partial(relax_kernel, lax.axis_size("by"), lax.axis_size("bz")),
+        out_shape=jax.ShapeDtypeStruct(u.shape, jnp.float32),
+        in_specs=[pl.BlockSpec(memory_space=pl.ANY), pl.BlockSpec(memory_space=pltpu.VMEM)],
+        out_specs=pl.BlockSpec(memory_space=pltpu.VMEM),
+        scratch_shapes=[
+            cells,
+            cells,
+            pltpu.VMEM((ny + 2, nz + 16, nx), jnp.float32),
+            pltpu.VMEM((2, nz, nx), jnp.float32),
+            pltpu.VMEM((2, nf + 1, ny, nx), jnp.float32),
+            pltpu.VMEM((2, nf + 1, ny, nx), jnp.float32),
+            pltpu.VMEM((2, nf, ny, nx), jnp.float32),
+            pltpu.VMEM((2, nf, ny, nx), jnp.float32),
+            pltpu.SemaphoreType.DMA,
+            pltpu.SemaphoreType.DMA((10,)),
+            pltpu.SemaphoreType.DMA((10,)),
+        ],
+        compiler_params=pltpu.CompilerParams(collective_id=1, has_side_effects=True, vmem_limit_bytes=VMEM_LIMIT),
+        name="relax",
+    )(u, k)
+
+
+def gram_kernel(total_rows, rows_ref, gram_ref, head, cross):
+    nx = rows_ref.shape[1]
     half = nx // 2
     tall = (((0,), (0,)), ((), ()))
-    head[...] = jnp.zeros_like(head)
-    cross[...] = jnp.zeros_like(cross)
-
-    def add(f, carry):
-        x = rows_ref[f].reshape(ny * nz, nx)
-        hi = x.astype(jnp.bfloat16)
-        lo = (x - hi.astype(jnp.float32)).astype(jnp.bfloat16)
-        for c in range(2):
-            cols = slice(c * half, (c + 1) * half)
-            left = hi[:, cols]
-            cross[cols, :] += lax.dot_general(left, lo, tall, preferred_element_type=jnp.float32)
-            head[cols, c * half :] += lax.dot_general(left, hi[:, c * half :], tall, preferred_element_type=jnp.float32)
-        return carry
-
-    lax.fori_loop(0, nf, add, 0)
-    for b, (i, j) in enumerate(upper_blocks(nx)):
-        ri, rj = slice(i * STEP, (i + 1) * STEP), slice(j * STEP, (j + 1) * STEP)
-        total = head[ri, rj] + (cross[ri, rj] + cross[rj, ri].T)
-        gram_ref[b * STEP : (b + 1) * STEP, :] = total / jnp.float32(total_rows)
-
-
-def relax_call(u, k, faces, kfaces, with_faces, total_rows=1):
-    nf, ny, nz, nx = u.shape
-    full = jax.ShapeDtypeStruct(u.shape, jnp.float32)
-    yface = jax.ShapeDtypeStruct((nf, nz, nx), jnp.float32)
-    zface = jax.ShapeDtypeStruct((nf, ny, nx), jnp.float32)
-    packed = jax.ShapeDtypeStruct((len(upper_blocks(nx)) * STEP, STEP), jnp.float32)
-    outs = [full] + ([yface, yface, zface, zface] if with_faces else [packed])
+    step = pl.program_id(0)
+
+    @pl.when(step == 0)
+    def _():
+        head[...] = jnp.zeros_like(head)
+        cross[...] = jnp.zeros_like(cross)
+
+    x = rows_ref[...]
+    hi = x.astype(jnp.bfloat16)
+    lo = (x - hi.astype(jnp.float32)).astype(jnp.bfloat16)
+    for c in range(2):
+        cols = slice(c * half, (c + 1) * half)
+        left = hi[:, cols]
+        cross[cols, :] += lax.dot_general(left, lo, tall, preferred_element_type=jnp.float32)
+        head[cols, c * half :] += lax.dot_general(left, hi[:, c * half :], tall, preferred_element_type=jnp.float32)
+
+    @pl.when(step == pl.num_programs(0) - 1)
+    def _():
+        for b, (i, j) in enumerate(upper_blocks(nx)):
+            ri, rj = slice(i * STEP, (i + 1) * STEP), slice(j * STEP, (j + 1) * STEP)
+            total = head[ri, rj] + (cross[ri, rj] + cross[rj, ri].T)
+            gram_ref[b * STEP : (b + 1) * STEP, :] = total / jnp.float32(total_rows)
+
+
+def gram_call(rows, total_rows, parts):
+    count, nx = rows.shape
+    packed = (len(upper_blocks(nx)) * STEP, STEP)
     return pl.pallas_call(
-        functools.partial(relax_kernel, with_faces, total_rows),
-        out_shape=outs,
-        in_specs=[pl.BlockSpec(memory_space=pltpu.VMEM)] * 10,
-        out_specs=[pl.BlockSpec(memory_space=pltpu.VMEM)] * len(outs),
-        scratch_shapes=[
-            pltpu.VMEM((nf, ny + 2, nz + 16, nx), jnp.float32),
-            pltpu.VMEM((ny + 2, nz + 16, nx), jnp.float32),
-        ]
-        + ([] if with_faces else [pltpu.VMEM((nx, nx), jnp.float32)] * 2),
+        functools.partial(gram_kernel, total_rows),
+        grid=(parts,),
+        out_shape=jax.ShapeDtypeStruct(packed, jnp.float32),
+        in_specs=[pl.BlockSpec((count // parts, nx), lambda i: (i, 0))],
+        out_specs=pl.BlockSpec(packed, lambda i: (0, 0)),
+        scratch_shapes=[pltpu.VMEM((nx, nx), jnp.float32)] * 2,
         compiler_params=pltpu.CompilerParams(vmem_limit_bytes=VMEM_LIMIT),
-        name="relax",
-    )(u, k, *faces, *kfaces)
+        name="gram",
+    )(rows)
 
 
 def tree_sum(terms):
@@ -321,19 +427,9 @@
 def on_device(fields, conductance):
     nf, ny, nz, nx = fields.shape
     total_rows = nf * ny * lax.axis_size("by") * nz * lax.axis_size("bz")
-    stacked = lambda f, k: jnp.concatenate([f, k[None]], axis=0)
-    yfaces = shift_faces(
-        (stacked(fields[:, 0], conductance[0]), stacked(fields[:, ny - 1], conductance[ny - 1])), "by"
-    )
-    zfaces = shift_faces(
-        (stacked(fields[:, :, 0], conductance[:, 0]), stacked(fields[:, :, nz - 1], conductance[:, nz - 1])), "bz"
-    )
-    faces = [a[:nf] for a in (*yfaces, *zfaces)]
-    kfaces = [a[nf] for a in (*yfaces, *zfaces)]
-    once, ylo, yhi, zlo, zhi = relax_call(fields, conductance, faces, kfaces, True)
-    again = (*shift_faces((ylo, yhi), "by"), *shift_faces((zlo, zhi), "bz"))
-    relaxed, packed = relax_call(once, conductance, again, kfaces, False, total_rows)
+    relaxed = relax_call(fields, conductance)
     rows = relaxed.reshape(-1, nx)
+    packed = gram_call(rows, total_rows, nf)
     factor, linv = factor_call(sum_call(packed), nx)
     basis = lax.dot_general(
         rows, linv, (((1,), (1,)), ((), ())), precision=HIGH, preferred_element_type=jnp.float32

time: 165 us -> 131 us (0.79)
  starting transfers between devices: 19.9 us -> 0 us
  waiting for transfers between devices: 16.1 us -> 0 us
  Pallas kernels: 103 us -> 119 us
  local copies, waits for them, and re-layouts: 12.8 us -> 0 us
    ppermute x8 -> x0, starting transfers between devices: 19.9 us -> none  [the longest x4 14.5 us: shift_faces(): below = lax.ppermute(tail, axis, [(i, i + 1) for i in range(count - 1)])]
    ppermute x8 -> x0, waiting for transfers between devices: 16.1 us -> none  [the longest x4 11.3 us: shift_faces(): below = lax.ppermute(tail, axis, [(i, i + 1) for i in range(count - 1)])]
    pallas_call x2, Pallas kernels: 37.7 us -> 52 us  [the longest x1 42.1 us: relax_call(): pl.pallas_call(functools.partial(relax_kernel, lax.axis_size('by'), lax.a...]
    slice x7 -> x0, local copies, waits for them, and re-layouts: 7.89 us -> none  [the longest x4 3.16 us: on_device(): faces = [a[:nf] for a in (*yfaces, *zfaces)]]
    squeeze x5 -> x0, local copies, waits for them, and re-layouts: 3.78 us -> none  [the longest x4 2.49 us: on_device(): kfaces = [a[nf] for a in (*yfaces, *zfaces)]]
  transfers between devices with their start and end apart: 8 -> 0, of which waited for: 3 -> 0; matrix products, arithmetic and copies ran while one was open for 4% -> 0% of each run, Pallas kernels for 0% -> 0%
where the time goes in v3:
time: 131 us
  Pallas kernels  119 us (91%)
  matrix products  11.4 us (9%)
    pallas_call x1, Pallas kernels, relax_call(): pl.pallas_call(functools.partial(relax_kernel, lax.axis_size('by'), lax.a...  42.1 us
    pallas_call x1, Pallas kernels, sum_call(): pl.pallas_call(functools.partial(sum_kernel, nby, nbz), out_shape=jax.Sha...  33.9 us
    pallas_call x1, Pallas kernels, factor_call(): pl.pallas_call(factor_kernel, out_shape=[shape, shape], in_specs=[pl.Bloc...  32.7 us
    dot_general x1, matrix products, on_device(): lax.dot_general(rows, linv, (((1,), (1,)), ((), ())), precision=HIGH, pre...  11.4 us
    pallas_call x1, Pallas kernels, gram_call(): pl.pallas_call(functools.partial(gram_kernel, total_rows), grid=(parts,),...  9.95 us

profile of v3, /device:TPU:0, one launch (start us, length us, event | category | flops | bytes accessed | tf_op | source)
XLA Modules:
  0.0 130.6 jit_solution(7818100885560399672)
XLA Ops:
  0.6 42.1 %relax.1 = f32[8,16,32,512]{3,2,1,0:T(8,128)} custom-call(f32[8,16,32,512]{3,2,1,0:T(8,128)} %u_ref.1, f32[16,32,512]{2,1,0:T(8,128)} %k_ref.1), custom_call_target="tpu_custom_call" | custom-call | tf_op jit(solution)/shard_map/relax/pallas_call | solution.py:180
  42.7 10.0 %gram.1.in_ref = f32[1280,128]{1,0:T(8,128)} custom-call(f32[4096,512]{1,0:T(8,128)} %bitcast.7), custom_call_target="tpu_custom_call" | custom-call | tf_op jit(solution)/shard_map/gram/pallas_call | solution.py:234
  52.7 33.9 %sum_all.1.gram_ref = f32[1280,128]{1,0:T(8,128)} custom-call(f32[1280,128]{1,0:T(8,128)} %gram.1.in_ref), custom_call_target="tpu_custom_call" | custom-call | tf_op jit(solution)/shard_map/sum_all/pallas_call | solution.py:411
  86.5 32.7 %factor.1 = (f32[512,512]{1,0:T(8,128)}, f32[512,512]{1,0:T(8,128)}) custom-call(f32[1280,128]{1,0:T(8,128)} %sum_all.1.gram_ref), custom_call_target="tpu_custom_call" | custom-call | tf_op jit(solution)/shard_map/factor/pallas_call | solution.py:328
  119.2 11.4 %fusion = f32[8,16,32,512]{3,2,1,0:T(8,128)} fusion(f32[8,16,32,512]{3,2,1,0:T(8,128)} %relax.1, f32[512,512]{1,0:T(8,128)} %get-tuple-element.4), kind=kOutput, calls=%fused_computation | convolution fusion | flops 6442450944 | bytes 17825792 | tf_op jit(solution)/shard_map/dot_general | solution.py:434

commit v4 on v3

--- a/solution.py
+++ b/solution.py
@@ -429,7 +429,7 @@
     total_rows = nf * ny * lax.axis_size("by") * nz * lax.axis_size("bz")
     relaxed = relax_call(fields, conductance)
     rows = relaxed.reshape(-1, nx)
-    packed = gram_call(rows, total_rows, nf)
+    packed = gram_call(rows, total_rows, max(nf // 2, 1))
     factor, linv = factor_call(sum_call(packed), nx)
     basis = lax.dot_general(
         rows, linv, (((1,), (1,)), ((), ())), precision=HIGH, preferred_element_type=jnp.float32

time: 131 us -> 129 us (0.985)
  Pallas kernels: 119 us -> 117 us
    pallas_call x1, Pallas kernels: 9.95 us -> 8.07 us  [gram_call(): pl.pallas_call(functools.partial(gram_kernel, total_rows), grid=(parts,),...]
where the time goes in v4:
time: 129 us
  Pallas kernels  117 us (91%)
  matrix products  11.4 us (9%)
    pallas_call x1, Pallas kernels, relax_call(): pl.pallas_call(functools.partial(relax_kernel, lax.axis_size('by'), lax.a...  42.1 us
    pallas_call x1, Pallas kernels, sum_call(): pl.pallas_call(functools.partial(sum_kernel, nby, nbz), out_shape=jax.Sha...  33.8 us
    pallas_call x1, Pallas kernels, factor_call(): pl.pallas_call(factor_kernel, out_shape=[shape, shape], in_specs=[pl.Bloc...  32.7 us
    dot_general x1, matrix products, on_device(): lax.dot_general(rows, linv, (((1,), (1,)), ((), ())), precision=HIGH, pre...  11.4 us
    pallas_call x1, Pallas kernels, gram_call(): pl.pallas_call(functools.partial(gram_kernel, total_rows), grid=(parts,),...  8.07 us

profile of v4, /device:TPU:0, one launch (start us, length us, event | category | flops | bytes accessed | tf_op | source)
XLA Modules:
  0.0 128.7 jit_solution(11483174347056990986)
XLA Ops:
  0.6 42.1 %relax.1 = f32[8,16,32,512]{3,2,1,0:T(8,128)} custom-call(f32[8,16,32,512]{3,2,1,0:T(8,128)} %u_ref.1, f32[16,32,512]{2,1,0:T(8,128)} %k_ref.1), custom_call_target="tpu_custom_call" | custom-call | tf_op jit(solution)/shard_map/relax/pallas_call | solution.py:180
  42.7 8.1 %gram.1.in_ref = f32[1280,128]{1,0:T(8,128)} custom-call(f32[4096,512]{1,0:T(8,128)} %bitcast.7), custom_call_target="tpu_custom_call" | custom-call | tf_op jit(solution)/shard_map/gram/pallas_call | solution.py:234
  50.8 33.8 %sum_all.1.gram_ref = f32[1280,128]{1,0:T(8,128)} custom-call(f32[1280,128]{1,0:T(8,128)} %gram.1.in_ref), custom_call_target="tpu_custom_call" | custom-call | tf_op jit(solution)/shard_map/sum_all/pallas_call | solution.py:411
  84.6 32.7 %factor.1 = (f32[512,512]{1,0:T(8,128)}, f32[512,512]{1,0:T(8,128)}) custom-call(f32[1280,128]{1,0:T(8,128)} %sum_all.1.gram_ref), custom_call_target="tpu_custom_call" | custom-call | tf_op jit(solution)/shard_map/factor/pallas_call | solution.py:328
  117.3 11.4 %fusion = f32[8,16,32,512]{3,2,1,0:T(8,128)} fusion(f32[8,16,32,512]{3,2,1,0:T(8,128)} %relax.1, f32[512,512]{1,0:T(8,128)} %get-tuple-element.4), kind=kOutput, calls=%fused_computation | convolution fusion | flops 6442450944 | bytes 17825792 | tf_op jit(solution)/shard_map/dot_general | solution.py:434
